TPU v7x, 256 devices: a whole 4x4x8 slice. The times are simulated.
256 devices in a mesh: dp: 64 (over y, z, core), grp: 4 (over x).
Axes of the slice: x: 4, y: 4, z: 8, core: 2. Of those that a mesh axis runs over, the one named last changes fastest.
Arguments:
- states: bfloat16 [32768, 1024], P('dp'), may hold values from -8 to 8
- w_up: bfloat16 [1024, 4096], P('dp', 'grp'), may hold values from -0.1875 to 0.1875
- w_down: bfloat16 [4096, 1024], P('grp', 'dp'), may hold values from -0.09375 to 0.09375
- gain: float32 [1024], replicated, may hold values from 0.5 to 1.5
- query_lengths: int32 [64, 8], P('dp'), may hold values from 1 to 32, as said below
- passage_lengths: int32 [64, 8], P('dp'), may hold values from 1 to 128, as said below
- positive: int32 [512], P('dp'), may hold values from 0 to 511, as said below
- negatives: int32 [512, 15], P('dp'), may hold values from 0 to 511
Outputs:
- loss: float32 [], replicated
- grad_up: float32 [1024, 4096], P('dp', 'grp')
- grad_down: float32 [4096, 1024], P('grp', 'dp')
- grad_gain: float32 [1024], replicated
Inputs may be any that keep to these rules, and one draw needn't show every extreme that they name: `query_lengths`: each row sums to 128. `passage_lengths`: each row sums to 384. Every passage is the positive of exactly one query, and it is held on a dp index other than that query's own. `negatives`: ids may repeat.
All inputs are finite; a program needn't handle non-finite values.
Results may differ from a plain program's by a relative error of at most 0.0029.
Values may be sent and summed in bfloat16 or wider, within the bound.
No kernel may reach another device: no remote copies, remote signals or barrier semaphores. Data moves between devices by JAX's collectives and lax.ppermute only.
A program may use at most 64 MiB of HBM per device.

v0:
```python
import functools

import jax
import jax.numpy as jnp
from jax import lax
from jax.experimental import pallas as pl
from jax.experimental.pallas import tpu as pltpu
from jax.sharding import Mesh, PartitionSpec as P

QTOK = 128
Y, Z, CORE, GRP = 4, 8, 2, 4
TEMPER = 0.02
EMBED_STEP = 1024.0
PARTIAL_STEP = 0.25
f32, bf16, f16 = jnp.float32, jnp.bfloat16, jnp.float16
EXACT = lax.Precision.HIGHEST
THREE = lax.Precision.HIGH


def normal_cdf(values):
    return 0.5 * (1.0 + lax.erf(values * 0.7071067811865476))


def gelu_exact(values):
    return values * normal_cdf(values)


def gelu_slope(values):
    return normal_cdf(values) + values * jnp.exp(-0.5 * values * values) * 0.3989422804014327


def segment_table(query_lengths, passage_lengths, total, shift):
    query_starts = jnp.cumsum(query_lengths) - query_lengths
    passage_starts = QTOK + jnp.cumsum(passage_lengths) - passage_lengths
    starts = jnp.concatenate([query_starts, passage_starts])
    lengths = jnp.concatenate([query_lengths, passage_lengths])
    places = ((jnp.arange(total, dtype=jnp.int32) + shift) % total)[:, None]
    inside = (places >= starts[None, :]) & (places < (starts + lengths)[None, :])
    return inside.astype(f32) / lengths.astype(f32)[None, :]


def spread(value, axis, count):
    return lax.all_to_all(jnp.broadcast_to(value[None], (count,) + value.shape), axis, 0, 0)


def other_core(value):
    return lax.ppermute(value, "core", [(0, 1), (1, 0)])


def shifted(value, axis, count, step):
    return lax.ppermute(value, axis, [(j, (j + step) % count) for j in range(count)])


def send_shifted(value, axis, count):
    return [shifted(value, axis, count, k) for k in range(1, count)]


def place_kernel(place, *refs):
    *pieces, out = refs
    count = len(pieces)
    for k, piece in enumerate(pieces):
        out[lax.rem(place[0] + count - k, count)] = piece[...]


def place_pieces(value, moved, axis):
    pieces = [value, *moved]
    vmem = pl.BlockSpec(memory_space=pltpu.VMEM)
    return pl.pallas_call(
        place_kernel,
        out_shape=jax.ShapeDtypeStruct((len(pieces),) + value.shape, value.dtype),
        in_specs=[pl.BlockSpec(memory_space=pltpu.SMEM)] + [vmem] * len(pieces),
        out_specs=vmem,
        compiler_params=pltpu.CompilerParams(vmem_limit_bytes=16 * 1024 * 1024),
        cost_estimate=pl.CostEstimate(flops=0, bytes_accessed=2**21, transcendentals=0),
    )(lax.axis_index(axis).reshape(1).astype(jnp.int32), *pieces)


def sum_permutes(value, axis, count):
    place = lax.axis_index(axis)
    moved = jnp.stack([value] + [shifted(value, axis, count, k) for k in range(1, count)])
    total = lax.dynamic_index_in_dim(moved, place, 0, keepdims=False)
    for k in range(1, count):
        total = total + lax.dynamic_index_in_dim(moved, (place - k) % count, 0, keepdims=False)
    return total


def dot_nt(a, b, precision=None):
    return lax.dot_general(
        a, b, (((1,), (1,)), ((), ())), precision=precision, preferred_element_type=f32
    )


def dot_tn(a, b, precision=None):
    return lax.dot_general(
        a, b, (((0,), (0,)), ((), ())), precision=precision, preferred_element_type=f32
    )


def split_high(value):
    high = value.astype(bf16)
    return high, (value - high.astype(f32)).astype(bf16)


def three_nn(a, high, low):
    a_high, a_low = split_high(a)
    dot = functools.partial(jnp.dot, preferred_element_type=f32)
    return dot(a_high, high[...]) + (dot(a_high, low[...]) + dot(a_low, high[...]))


def loss_kernel(
    scalars, first, second, embed, scale, gain,
    d_logits, loss, d_sums, q_high, q_low, p_high, p_low, logits, times, ids,
):
    core, block = scalars[0], scalars[1]
    half_count = first.shape[0] * 8
    count, width = q_high.shape
    half = width // 2
    listed = ids.shape[0]

    def split(i, carry):
        for source, base in ((first, 0), (second, half_count)):
            rows = pl.ds(pl.multiple_of(base + 16 * i, 16), 16)
            for offset, high, low in ((0, q_high, q_low), (8, p_high, p_low)):
                value = source[pl.ds(2 * i, 2), offset : offset + 8, :width].reshape(16, width)
                high[rows, :], low[rows, :] = split_high(value)
        return carry

    lax.fori_loop(0, half_count // 16, split, 0)
    lanes = [source[:, 0:8, width:].reshape(half_count, 128) for source in (first, second)]
    ids[...] = jnp.concatenate(lanes, axis=0).T[:listed]

    to_logits = 1.0 / (TEMPER * EMBED_STEP * EMBED_STEP)
    raw = dot_nt(p_high[...], q_high[...])
    raw = raw + (dot_nt(p_high[...], q_low[...]) + dot_nt(p_low[...], q_high[...]))
    logits[...] = raw * to_logits

    step = 32
    columns = lax.broadcasted_iota(jnp.int32, (step, count), 1) >> 3
    offsets = lax.broadcasted_iota(jnp.int32, (step, count), 0)

    def fold(value):
        return value.reshape(step // 8, 8, count)

    def count_times(i, carry):
        top, named = carry
        rows = pl.ds(pl.multiple_of(i * step, step), step)
        places = offsets + i * step
        whole = places.astype(f32)
        is_first = whole == ids[0:1, :]
        total = jnp.where(is_first, 1.0, 0.0) + jnp.where((places >> 3) == columns, 1.0, 0.0)
        for k in range(1, listed):
            total = total + jnp.where(whole == ids[k : k + 1, :], 1.0, 0.0)
        value = logits[rows, :]
        times[rows, :] = total
        top = jnp.maximum(top, jnp.max(fold(jnp.where(total > 0.0, value, -1e30)), axis=0))
        return top, named + jnp.sum(fold(jnp.where(is_first, value, 0.0)), axis=0)

    start = (jnp.full((8, count), -1e30, f32), jnp.zeros((8, count), f32))
    top, named = lax.fori_loop(0, count // step, count_times, start)
    top = jnp.max(top, axis=0, keepdims=True)
    named = jnp.sum(named, axis=0, keepdims=True)

    def weigh(i, carry):
        rows = pl.ds(pl.multiple_of(i * step, step), step)
        total = times[rows, :]
        weight = total * jnp.exp(jnp.where(total > 0.0, logits[rows, :] - top, 0.0))
        times[rows, :] = weight
        return carry + jnp.sum(fold(weight), axis=0)

    total = lax.fori_loop(0, count // step, weigh, jnp.zeros((8, count), f32))
    total = jnp.sum(total, axis=0, keepdims=True)
    loss[...] = jnp.broadcast_to(
        jnp.sum(jnp.log(total) + top - named, axis=1, keepdims=True) / count, loss.shape
    )
    share = 1.0 / total

    def differ(i, carry):
        rows = pl.ds(pl.multiple_of(i * step, step), step)
        is_first = (offsets + i * step).astype(f32) == ids[0:1, :]
        d_logits[rows, :] = times[rows, :] * share - jnp.where(is_first, 1.0, 0.0)
        return carry

    lax.fori_loop(0, count // step, differ, 0)

    own_place = block * 8
    picks = lax.broadcasted_iota(jnp.int32, (16, count), 0)
    picks = (lax.broadcasted_iota(jnp.int32, (16, count), 1) == picks + own_place) & (picks < 8)
    picks = jnp.where(picks, 1.0, 0.0).astype(bf16)
    d_high, d_low = split_high(d_logits[...])
    own_queries = dot_nt(picks, d_high) + dot_nt(picks, d_low)
    own_passages = d_logits[pl.ds(pl.multiple_of(own_place, 8), 8), :]
    own_passages = jnp.concatenate([own_passages, jnp.zeros_like(own_passages)], axis=0)
    d_embed = jnp.concatenate(
        [
            three_nn(own_queries, p_high, p_low)[:8],
            three_nn(own_passages, q_high, q_low)[:8],
        ],
        axis=0,
    ) * (1.0 / (TEMPER * EMBED_STEP))
    turned = jnp.concatenate([d_embed[:, half:], d_embed[:, :half]], axis=1)
    d_embed = jnp.where(core == 0, d_embed, turned)
    owned = embed[...]
    inner = jnp.sum(owned * d_embed, axis=1, keepdims=True)
    d_sums[...] = scale[...] * (d_embed - owned * inner) * gain[...]


def back_kernel(
    d_sums, table, own, next1, next2, next3, down_mine, down_theirs, slope,
    d_upward, mine_turned, theirs_turned,
):
    half = mine_turned.shape[0]
    value_high, value_low = split_high(d_sums[...])
    dot = functools.partial(jnp.dot, preferred_element_type=f32)
    for k, source in enumerate((own, next1, next2, next3)):
        size = source.shape[0]
        places = slice(k * size, (k + 1) * size)
        centred = source[...].astype(f32)
        inverse = lax.rsqrt(jnp.mean(centred * centred, axis=1, keepdims=True) + 1e-05)
        normed = centred * inverse
        part_high, part_low = split_high(table[places, :])
        d_normed = dot(part_high, value_high) + (
            dot(part_high, value_low) + dot(part_low, value_high)
        )
        d_mixed = inverse * (
            d_normed
            - jnp.mean(d_normed, axis=1, keepdims=True)
            - normed * jnp.mean(d_normed * normed, axis=1, keepdims=True)
        )
        d_hidden = dot(d_mixed[:, :half].astype(bf16), down_mine[...])
        d_hidden = d_hidden + dot(d_mixed[:, half:].astype(bf16), down_theirs[...])
        d_upward[places, :] = (d_hidden * slope[places, :]).astype(bf16)
        mine_turned[:, places] = d_mixed[:, :half].T.astype(bf16)
        theirs_turned[:, places] = d_mixed[:, half:].T.astype(bf16)


def own_kernel(a, b, c, d, up, down):
    step = 128
    for row in range(0, up.shape[0], step):
        rows = slice(row, row + step)
        up[rows, :] = dot_tn(a[:, rows], b[...])
        down[rows, :] = jnp.dot(c[rows, :], d[...], preferred_element_type=f32)


def other_kernel(up, down, a, b, c, d, out):
    out[0, 0] = (up[...] + dot_tn(a[...], b[...])).astype(bf16)
    out[0, 1] = (down[...] + jnp.dot(c[...], d[...], preferred_element_type=f32)).astype(bf16)


def own_gradients(states, d_upward, d_turned, hidden):
    vmem = pl.BlockSpec(memory_space=pltpu.VMEM)
    shape = jax.ShapeDtypeStruct((d_turned.shape[0], hidden.shape[1]), f32)
    return pl.pallas_call(
        own_kernel,
        out_shape=(shape, shape),
        in_specs=[vmem] * 4,
        out_specs=(vmem, vmem),
        compiler_params=pltpu.CompilerParams(vmem_limit_bytes=24 * 1024 * 1024),
        cost_estimate=pl.CostEstimate(flops=2**31, bytes_accessed=2**16, transcendentals=0),
    )(states, d_upward, d_turned, hidden)


def all_gradients(up, down, states, d_upward, d_turned, hidden):
    step, columns = up.shape[0] // Y, up.shape[1]
    vmem = pl.BlockSpec(memory_space=pltpu.VMEM)
    rows = pl.BlockSpec((step, columns), lambda k: (k, 0))
    return pl.pallas_call(
        other_kernel,
        grid=(Y,),
        out_shape=jax.ShapeDtypeStruct((Y, 2, step, columns), bf16),
        in_specs=[
            rows,
            rows,
            pl.BlockSpec((states.shape[0], step), lambda k: (0, k)),
            vmem,
            pl.BlockSpec((step, d_turned.shape[1]), lambda k: (k, 0)),
            vmem,
        ],
        out_specs=pl.BlockSpec((1, 2, step, columns), lambda k: (k, 0, 0, 0)),
        compiler_params=pltpu.CompilerParams(vmem_limit_bytes=24 * 1024 * 1024),
        cost_estimate=pl.CostEstimate(flops=2**31, bytes_accessed=2**22, transcendentals=0),
    )(up, down, states, d_upward, d_turned, hidden)


def scale_kernel(moved, out):
    owned = out.shape[1] // 2
    width = moved.shape[3]
    for z in range(out.shape[0]):
        for part in range(2):
            rows = slice(z * owned, (z + 1) * owned)
            total = moved[0, part, rows, :].astype(f32)
            for k in range(1, moved.shape[0]):
                total = total + moved[k, part, rows, :].astype(f32)
            largest = jnp.max(jnp.abs(total), axis=1, keepdims=True)
            exponent = jnp.floor(jnp.log(jnp.maximum(largest, 1e-30)) * 1.4426950408889634)
            places = slice(part * owned, (part + 1) * owned)
            out[z, places, :width] = total * jnp.exp(exponent * -0.6931471805599453)
            out[z, places, width:] = jnp.broadcast_to(exponent, (owned, 128))


def scale_rows(moved):
    count, parts, rows, columns = moved.shape
    vmem = pl.BlockSpec(memory_space=pltpu.VMEM)
    return pl.pallas_call(
        scale_kernel,
        out_shape=jax.ShapeDtypeStruct((Z, parts * rows // Z, columns + 128), f32),
        in_specs=[vmem],
        out_specs=vmem,
        compiler_params=pltpu.CompilerParams(vmem_limit_bytes=16 * 1024 * 1024),
        cost_estimate=pl.CostEstimate(flops=2**20, bytes_accessed=2**22, transcendentals=0),
    )(moved)


def all_losses(scalars, first, second, embed, scale, gain, listed):
    count, width = first.shape[0] * 16, embed.shape[1]
    vmem = pl.BlockSpec(memory_space=pltpu.VMEM)
    return pl.pallas_call(
        loss_kernel,
        out_shape=(
            jax.ShapeDtypeStruct((count, count), f32),
            jax.ShapeDtypeStruct((8, 128), f32),
            jax.ShapeDtypeStruct(embed.shape, f32),
        ),
        in_specs=[pl.BlockSpec(memory_space=pltpu.SMEM)] + [vmem] * 5,
        out_specs=(vmem,) * 3,
        scratch_shapes=[pltpu.VMEM((count, width), bf16)] * 4
        + [pltpu.VMEM((count, count), f32)] * 2
        + [pltpu.VMEM((listed, count), f32)],
        compiler_params=pltpu.CompilerParams(vmem_limit_bytes=40 * 1024 * 1024),
        cost_estimate=pl.CostEstimate(flops=2**20, bytes_accessed=2**16, transcendentals=0),
    )(scalars, first, second, embed, scale, gain)


def norm_back(d_sums, table, quarters, down_mine, down_theirs, slope):
    tokens, half = table.shape[0], d_sums.shape[1] // 2
    vmem = pl.BlockSpec(memory_space=pltpu.VMEM)
    return pl.pallas_call(
        back_kernel,
        out_shape=(jax.ShapeDtypeStruct(slope.shape, bf16),)
        + (jax.ShapeDtypeStruct((half, tokens), bf16),) * 2,
        in_specs=[vmem] * (5 + len(quarters)),
        out_specs=(vmem,) * 3,
        compiler_params=pltpu.CompilerParams(vmem_limit_bytes=24 * 1024 * 1024),
        cost_estimate=pl.CostEstimate(flops=2**20, bytes_accessed=2**16, transcendentals=0),
    )(d_sums, table, *quarters, down_mine, down_theirs, slope)


def shards(states, w_up, w_down, gain, query_lengths, passage_lengths, positive, negatives):
    tokens, width = states.shape
    half = width // 2
    owned = w_up.shape[0]
    quarter = tokens // GRP
    queries = positive.shape[0]
    core = lax.axis_index("core")
    member = lax.axis_index("grp")
    block = core * (Y * Z) + lax.axis_index("y") * Z + lax.axis_index("z")

    def swap_halves(value):
        return jnp.where(core == 0, value, jnp.roll(value, half, axis=-1))

    def turn(value):
        parts = value.reshape((GRP, quarter) + value.shape[1:])
        order = [lax.dynamic_index_in_dim(parts, (member + k) % GRP, 0, keepdims=False) for k in range(GRP)]
        return jnp.concatenate(order, axis=0)

    cores = turn(states).reshape(tokens, Y * Z, CORE, owned).transpose(2, 0, 1, 3).reshape(CORE, tokens, half)
    states_mine = lax.dynamic_index_in_dim(cores, core, 0, keepdims=False)
    states_theirs = lax.dynamic_index_in_dim(cores, 1 - core, 0, keepdims=False)
    gain_common = gain.reshape(Y * Z, CORE, owned).transpose(1, 0, 2).reshape(1, width)
    gain_local = swap_halves(gain_common)

    up_z = spread(w_up, "z", Z)
    up_z, states_mine, states_theirs, down_sent = lax.optimization_barrier(
        (up_z, states_mine, states_theirs, w_down.T)
    )
    down_z = spread(down_sent, "z", Z)
    up_moved = send_shifted(up_z, "y", Y)
    up_moved, down_z = lax.optimization_barrier((up_moved, down_z))
    up_mine = place_pieces(up_z, up_moved, "y").reshape(half, -1)
    up_theirs = other_core(up_mine)
    down_moved = send_shifted(down_z, "y", Y)
    states_sent = other_core(states_theirs)

    upward = jnp.dot(states_mine, up_mine, preferred_element_type=f32) + jnp.dot(
        states_theirs, up_theirs, preferred_element_type=f32
    )
    hidden = gelu_exact(upward).astype(bf16)
    hidden, down_moved = lax.optimization_barrier((hidden, down_moved))
    hidden_sent = other_core(hidden)
    down_mine = place_pieces(down_z, down_moved, "y").reshape(half, -1)
    down_theirs = other_core(down_mine)
    down = jnp.concatenate([down_mine, down_theirs], axis=0)

    partial = (dot_nt(hidden[quarter:], down) * PARTIAL_STEP).astype(f16)
    arrived = [
        shifted(partial[(k - 1) * quarter : k * quarter], "grp", GRP, k) for k in range(1, GRP)
    ]
    mixed = jnp.concatenate([states_mine[:quarter], states_theirs[:quarter]], axis=1).astype(f32)
    mixed = mixed + dot_nt(hidden[:quarter], down)
    for piece in arrived:
        mixed = mixed + piece.astype(f32) * (1.0 / PARTIAL_STEP)
    centred = mixed - jnp.mean(mixed, axis=-1, keepdims=True)
    inverse = lax.rsqrt(jnp.mean(centred * centred, axis=-1, keepdims=True) + 1e-05)
    normed = centred * inverse
    table = segment_table(query_lengths[0], passage_lengths[0], tokens, member * quarter)
    pooled = sum_permutes(dot_tn(table[:quarter], normed, EXACT), "grp", GRP) * gain_local
    scale = lax.rsqrt(jnp.sum(pooled * pooled, axis=-1, keepdims=True) + 1e-06)
    embed = pooled * scale

    centred_sent = centred.astype(bf16)
    quarters = [centred_sent] + [shifted(centred_sent, "grp", GRP, GRP - k) for k in range(1, GRP)]
    slope = gelu_slope(upward)

    listed = jnp.concatenate([positive[:, None], negatives], axis=1)
    owner = listed // queries
    listed = ((owner % CORE) * (Y * Z) + owner // CORE) * queries + listed % queries
    lanes = jnp.pad(listed.astype(f32), ((0, queries), (0, 128 - listed.shape[1])))
    sent = jnp.concatenate([swap_halves(embed) * EMBED_STEP, lanes], axis=1).astype(f16)
    mine = spread(sent, "z", Z)
    mine, slope = lax.optimization_barrier((mine, slope))
    mine = spread(mine, "y", Y)
    mine, *quarters = lax.optimization_barrier((mine, *quarters))
    theirs = other_core(mine)
    first = jnp.where(core == 0, mine, theirs).astype(f32).reshape(Y * Z, 2 * queries, width + 128)
    second = jnp.where(core == 0, theirs, mine).astype(f32).reshape(Y * Z, 2 * queries, width + 128)
    d_logits, loss, d_sums = all_losses(
        jnp.stack([core, block]).astype(jnp.int32), first, second, embed, scale, gain_local,
        listed.shape[1],
    )
    d_upward, mine_turned, theirs_turned = norm_back(
        d_sums, table, quarters, down_mine, down_theirs, slope
    )

    d_sent = other_core(theirs_turned)
    d_upward_sent = other_core(d_upward)
    up_own, down_own = own_gradients(states_mine, d_upward, mine_turned, hidden)
    pieces = all_gradients(up_own, down_own, states_sent, d_upward_sent, d_sent, hidden_sent)
    last = scale_rows(lax.all_to_all(pieces, "y", 0, 0)).astype(f16)
    last = lax.all_to_all(last, "z", 0, 0)
    factor = jnp.exp2(last[..., width : width + 1].astype(f32))
    last = jnp.sum(last[..., :width].astype(f32) * factor, axis=0)
    grad_up = last[:owned]
    grad_down = last[owned:].T

    d_logits, first, second, _ = lax.optimization_barrier((d_logits, first, second, pieces))
    both = jnp.concatenate([first, second], axis=0)[:, :, :width]
    all_queries = both[:, :queries].reshape(-1, width) * (1.0 / EMBED_STEP)
    all_passages = both[:, queries:].reshape(-1, width) * (1.0 / EMBED_STEP)
    drawn = jnp.dot(d_logits, all_queries, precision=THREE)
    product = drawn * all_passages
    from_passages = jnp.sum(product, axis=1, keepdims=True)
    from_queries = jnp.sum(
        dot_tn(d_logits, all_passages, THREE) * all_queries, axis=1, keepdims=True
    )
    grad_gain = (
        2.0 * jnp.sum(product, axis=0)
        - jnp.sum(from_queries * all_queries * all_queries, axis=0)
        - jnp.sum(from_passages * all_passages * all_passages, axis=0)
    ) / TEMPER / gain_common[0]
    grad_gain = grad_gain.reshape(CORE, Y * Z, owned).transpose(1, 0, 2).reshape(width)
    return (loss[0, 0], grad_up, grad_down, grad_gain)


def solution(mesh):
    split = Mesh(mesh.devices.reshape(Y, Z, CORE, GRP), ("y", "z", "core", "grp"))
    dp = ("y", "z", "core")
    return jax.shard_map(
        shards,
        mesh=split,
        in_specs=(
            P(dp, None),
            P(dp, "grp"),
            P("grp", dp),
            P(),
            P(dp, None),
            P(dp, None),
            P(dp),
            P(dp, None),
        ),
        out_specs=(P(), P(dp, "grp"), P("grp", dp), P()),
        check_vma=False,
    )
```

profile of v0, /device:TPU:1, one launch (start us, length us, event | category | flops | bytes accessed | tf_op | source)
XLA Modules:
  0.0 213.4 jit_solution(12929237248591240858)
XLA Ops:
  2.1 9.0 %all-to-all-start = ((bf16[8,16,1024]{2,1,0:T(8,128)(2,1)}), bf16[8,16,1024]{2,1,0:T(8,128)(2,1)S(1)}, u32[]{:S(2)}, u32[]{:S(2)}) async-start(bf16[8,16,1024]{2,1,0:T(8,128)(2,1)} %broadcast_in_dim.10), calls=%async_computation | async-start | bytes 524288 | tf_op jit(solution)/shard_map/all_to_all | solution.py:43
  13.9 7.6 %all-to-all-done.refs_0_ = bf16[8,16,1024]{2,1,0:T(8,128)(2,1)S(1)} async-done(((bf16[8,16,1024]{2,1,0:T(8,128)(2,1)}), bf16[8,16,1024]{2,1,0:T(8,128)(2,1)S(1)}, u32[]{:S(2)}, u32[]{:S(2)}) %all-to-all-start) | async-done | bytes 262176 | tf_op jit(solution)/shard_map/all_to_all | solution.py:43
  22.2 3.4 %all-to-all-start.1 = ((bf16[8,16,1024]{2,1,0:T(8,128)(2,1)}), bf16[8,16,1024]{2,1,0:T(8,128)(2,1)S(1)}, u32[]{:S(2)}, u32[]{:S(2)}) async-start(bf16[8,16,1024]{2,1,0:T(8,128)(2,1)} %broadcast_in_dim.11), calls=%async_computation.1 | async-start | bytes 524288 | tf_op jit(solution)/shard_map/all_to_all | solution.py:43
  27.0 2.6 %collective-permute-start.1 = (bf16[8,16,1024]{2,1,0:T(8,128)(2,1)S(1)}, bf16[8,16,1024]{2,1,0:T(8,128)(2,1)S(1)}, u32[]{:S(2)}, u32[]{:S(2)}) collective-permute-start(bf16[8,16,1024]{2,1,0:T(8,128)(2,1)S(1)} %all-to-all-done.refs_0_), channel_id=1, source_target_pairs={{0,128},{64,192},{128,0},{192,64},{1,129},{65,193},{129,1},{193,65... | collective-permute-start | bytes 786440 | tf_op jit(solution)/shard_map/ppermute | solution.py:51
  32.2 6.6 %collective-permute-done.1.refs_2_ = bf16[8,16,1024]{2,1,0:T(8,128)(2,1)S(1)} collective-permute-done((bf16[8,16,1024]{2,1,0:T(8,128)(2,1)S(1)}, bf16[8,16,1024]{2,1,0:T(8,128)(2,1)S(1)}, u32[]{:S(2)}, u32[]{:S(2)}) %collective-permute-start.1) | collective-permute-done | bytes 262176 | tf_op jit(solution)/shard_map/ppermute | solution.py:51
  39.1 3.6 %collective-permute-start.3 = (bf16[512,1024]{1,0:T(8,128)(2,1)S(1)}, bf16[512,1024]{1,0:T(8,128)(2,1)S(1)}, u32[]{:S(2)}, u32[]{:S(2)}) collective-permute-start(bf16[512,1024]{1,0:T(8,128)(2,1)S(1)} %bitcast.94), channel_id=1, source_target_pairs={{0,4},{4,0},{1,5},{5,1},{2,6},{6,2},{3,7},{7,3},{8,12},{12,8},{9,1... | collective-permute-start | bytes 3145736 | tf_op jit(solution)/shard_map/ppermute | solution.py:47
  44.3 2.1 collective-permute-start.5
  48.4 2.8 %fusion.3 = (f32[512,1024]{1,0:T(8,128)}, bf16[512,1024]{1,0:T(8,128)(2,1)}) fusion(f32[512,1024]{1,0:T(8,128)S(1)} %fusion.60, bf16[512,512]{1,0:T(8,128)(2,1)S(1)} %bitcast.109, bf16[512,1024]{1,0:T(8,128)(2,1)S(1)} %collective-permute-done.3), kind=kOutput, calls=%fused_computation.4 | convolution fusion | flops 542638080 | bytes 6815744 | tf_op jit(solution)/shard_map/dot_general | solution.py:383
  52.5 6.0 %collective-permute-done.5.refs_2_ = bf16[8,16,1024]{2,1,0:T(8,128)(2,1)S(1)} collective-permute-done((bf16[8,16,1024]{2,1,0:T(8,128)(2,1)S(1)}, bf16[8,16,1024]{2,1,0:T(8,128)(2,1)S(1)}, u32[]{:S(2)}, u32[]{:S(2)}) %collective-permute-start.5) | collective-permute-done | bytes 262176 | tf_op jit(solution)/shard_map/ppermute | solution.py:51
  59.8 2.1 %collective-permute-done.7.down_theirs = bf16[512,1024]{1,0:T(8,128)(2,1)S(1)} collective-permute-done((bf16[512,1024]{1,0:T(8,128)(2,1)S(1)}, bf16[512,1024]{1,0:T(8,128)(2,1)S(1)}, u32[]{:S(2)}, u32[]{:S(2)}) %collective-permute-start.7) | collective-permute-done | bytes 1048608 | tf_op jit(solution)/shard_map/ppermute | solution.py:47
  62.0 2.5 %multiply_convert_fusion.1 = f16[384,1024]{1,0:T(8,128)(2,1)S(1)} fusion(bf16[512,1024]{1,0:T(8,128)(2,1)S(1)} %collective-permute-done.7.down_theirs, bf16[512,1024]{1,0:T(8,128)(2,1)S(1)} %bitcast.97, bf16[512,1024]{1,0:T(8,128)(2,1)} %get-tuple-element.42.d), kind=kOutput, calls=%fused_computation.20 | convolution fusion | flops 810287104 | bytes 3670016 | tf_op jit(solution)/shard_map/dot_general | solution.py:88
  65.4 2.5 %collective-permute-start.10 = (f16[128,1024]{1,0:T(8,128)(2,1)}, f16[128,1024]{1,0:T(8,128)(2,1)}, u32[]{:S(2)}, u32[]{:S(2)}) collective-permute-start(f16[128,1024]{1,0:T(8,128)(2,1)} %get-tuple-element.81), channel_id=1, source_target_pairs={{0,3},{1,0},{2,1},{3,2},{4,7},{5,4},{6,5},{7,6},{8,11},{9,8},{10,9... | collective-permute-start | bytes 786440 | tf_op jit(solution)/shard_map/ppermute | solution.py:51
  69.4 9.6 %collective-permute-done.10 = f16[128,1024]{1,0:T(8,128)(2,1)} collective-permute-done((f16[128,1024]{1,0:T(8,128)(2,1)}, f16[128,1024]{1,0:T(8,128)(2,1)}, u32[]{:S(2)}, u32[]{:S(2)}) %collective-permute-start.10) | collective-permute-done | bytes 262176 | tf_op jit(solution)/shard_map/ppermute | solution.py:51
  79.0 4.6 %collective-permute-done.8 = f16[128,1024]{1,0:T(8,128)(2,1)} collective-permute-done((f16[128,1024]{1,0:T(8,128)(2,1)S(1)}, f16[128,1024]{1,0:T(8,128)(2,1)}, u32[]{:S(2)}, u32[]{:S(2)}) %collective-permute-start.8) | collective-permute-done | bytes 262176 | tf_op jit(solution)/shard_map/ppermute | solution.py:51
  83.6 2.2 %fusion.59 = (f32[128]{0:T(128)S(1)}, f32[128,1024]{1,0:T(8,128)S(1)}) fusion(f16[128,1024]{1,0:T(8,128)(2,1)} %collective-permute-done.10, f16[128,1024]{1,0:T(8,128)(2,1)} %collective-permute-done.9, f16[128,1024]{1,0:T(8,128)(2,1)} %collective-permute-done.8, bf16[512,1024]{1,0:T(8,128)(2,1)S(1)} %collective-permute-done.7.down_theirs, ...), kind=kOutput, calls=%fused_computation.127 | convolution fusion | flops 274595712 | bytes 3932672 | tf_op jit(solution)/shard_map/dot_general | solution.py:88
  92.8 15.6 %all_to_all.30 = f16[8,16,1152]{2,1,0:T(8,128)(2,1)S(1)} all-to-all(f16[8,16,1152]{2,1,0:T(8,128)(2,1)S(1)} %broadcast_in_dim.13), channel_id=1, replica_groups=mesh['y'=4,'z'=8,'core'=2,'grp'=4] {'z'}, dimensions={0} | all-to-all | bytes 589824 | tf_op jit(solution)/shard_map/all_to_all | solution.py:43
  109.5 3.6 %all-to-all-start.3 = ((f16[4,8,16,1152]{3,2,1,0:T(8,128)(2,1)}), f16[4,8,16,1152]{3,2,1,0:T(8,128)(2,1)S(1)}, u32[]{:S(2)}, u32[]{:S(2)}) async-start(f16[4,8,16,1152]{3,2,1,0:T(8,128)(2,1)} %broadcast_in_dim.14), calls=%async_computation.3 | async-start | bytes 2359296 | tf_op jit(solution)/shard_map/all_to_all | solution.py:43
  116.0 5.6 %collective-permute-done.14.next1 = bf16[128,1024]{1,0:T(8,128)(2,1)S(1)} collective-permute-done((bf16[128,1024]{1,0:T(8,128)(2,1)S(1)}, bf16[128,1024]{1,0:T(8,128)(2,1)S(1)}, u32[]{:S(2)}, u32[]{:S(2)}) %collective-permute-start.14) | collective-permute-done | bytes 262176 | tf_op jit(solution)/shard_map/ppermute | solution.py:51
  122.7 3.1 %collective-permute-done.16.next3 = bf16[128,1024]{1,0:T(8,128)(2,1)S(1)} collective-permute-done((bf16[128,1024]{1,0:T(8,128)(2,1)S(1)}, bf16[128,1024]{1,0:T(8,128)(2,1)S(1)}, u32[]{:S(2)}, u32[]{:S(2)}) %collective-permute-start.16) | collective-permute-done | bytes 262176 | tf_op jit(solution)/shard_map/ppermute | solution.py:51
  126.5 5.0 %collective-permute-start.17 = (f16[4,8,16,1152]{3,2,1,0:T(8,128)(2,1)S(1)}, f16[4,8,16,1152]{3,2,1,0:T(8,128)(2,1)}, u32[]{:S(2)}, u32[]{:S(2)}) collective-permute-start(f16[4,8,16,1152]{3,2,1,0:T(8,128)(2,1)S(1)} %all-to-all-done.3), channel_id=1, source_target_pairs={{0,4},{4,0},{1,5},{5,1},{2,6},{6,2},{3,7},{7,3},{8,12},{12,8},{9,1... | collective-permute-start | bytes 3538952 | tf_op jit(solution)/shard_map/ppermute | solution.py:47
  132.0 2.1 %collective-permute-done.17 = f16[4,8,16,1152]{3,2,1,0:T(8,128)(2,1)} collective-permute-done((f16[4,8,16,1152]{3,2,1,0:T(8,128)(2,1)S(1)}, f16[4,8,16,1152]{3,2,1,0:T(8,128)(2,1)}, u32[]{:S(2)}, u32[]{:S(2)}) %collective-permute-start.17) | collective-permute-done | bytes 1179680 | tf_op jit(solution)/shard_map/ppermute | solution.py:47
  136.5 7.1 %shard_map.113 = (f32[512,512]{1,0:T(8,128)S(1)}, f32[8,128]{1,0:T(8,128)S(1)}, f32[16,1024]{1,0:T(8,128)S(1)}) custom-call(s32[2]{0:T(128)S(1)} %pad_add_fusion.1.scalars, f32[32,16,1152]{2,1,0:T(8,128)S(1)} %bitcast_convert_fusion.1.first, f32[32,16,1152]{2,1,0:T(8,128)S(1)} %bitcast_convert_fusion.second, f32[16,1024]{1,0:T(8,128)S(1)} %fusion.31.embed, ...), custom_call_target="tpu_custom_call" | custom-call | flops 1048576 | bytes 65536 | tf_op jit(solution)/shard_map/pallas_call | solution.py:316
  143.8 3.0 %shard_map.114 = (bf16[512,1024]{1,0:T(8,128)(2,1)S(1)}, bf16[512,512]{1,0:T(8,128)(2,1)S(1)}, bf16[512,512]{1,0:T(8,128)(2,1)S(1)}) custom-call(f32[16,1024]{1,0:T(8,128)S(1)} %get-tuple-element.49.d_sums, f32[512,16]{1,0:T(8,128)S(1)} %copy-done.7, bf16[128,1024]{1,0:T(8,128)(2,1)S(1)} %copy-done.9, bf16[128,1024]{1,0:T(8,128)(2,1)S(1)} %copy-done.13, ...), custom_call_target="tpu_custom_call" | custom-call | flops 1048576 | bytes 65536 | tf_op jit(solution)/shard_map/pallas_call | solution.py:336
  147.8 2.5 %shard_map.115 = (f32[512,1024]{1,0:T(8,128)S(1)}, f32[512,1024]{1,0:T(8,128)S(1)}) custom-call(bf16[512,512]{1,0:T(8,128)(2,1)S(1)} %bitcast.102, bf16[512,1024]{1,0:T(8,128)(2,1)S(1)} %get-tuple-element.55.b, bf16[512,512]{1,0:T(8,128)(2,1)S(1)} %get-tuple-element.56.c, bf16[512,1024]{1,0:T(8,128)(2,1)} %get-tuple-element.42.d), custom_call_target="tpu_custom_call" | custom-call | flops 2147483648 | bytes 65536 | tf_op jit(solution)/shard_map/pallas_call | solution.py:252
  151.1 3.2 %shard_map.116 = bf16[4,2,128,1024]{3,2,1,0:T(8,128)(2,1)S(1)} custom-call(f32[512,1024]{1,0:T(8,128)S(1)} %get-tuple-element.57.up, f32[512,1024]{1,0:T(8,128)S(1)} %get-tuple-element.58.down, bf16[512,512]{1,0:T(8,128)(2,1)S(1)} %collective-permute-done.18.a, bf16[512,1024]{1,0:T(8,128)(2,1)S(1)} %collective-permute-done.19.b, ...), custom_call_target="tpu_custom_call" | custom-call | flops 2147483648 | bytes 4194304 | tf_op jit(solution)/shard_map/pallas_call | solution.py:266
  155.7 4.8 %all-to-all-start.4 = ((bf16[4,2,128,1024]{3,2,1,0:T(8,128)(2,1)}), bf16[4,2,128,1024]{3,2,1,0:T(8,128)(2,1)}, u32[]{:S(2)}, u32[]{:S(2)}) async-start(bf16[4,2,128,1024]{3,2,1,0:T(8,128)(2,1)} %copy-done.2), calls=%async_computation.4 | async-start | bytes 4194304 | tf_op jit(solution)/shard_map/all_to_all | solution.py:437
  163.9 2.2 %fusion.8 = f32[512]{0:T(512)S(1)} fusion(f32[512,512]{1,0:T(8,128)S(1)} %copy-done.19, f32[64,16,1152]{2,1,0:T(8,128)S(1)} %constant_dynamic-update-slice_fusion), kind=kOutput, calls=%fused_computation.12 | convolution fusion | flops 1612709376 | bytes 5244928 | tf_op jit(solution)/shard_map/dot_general | solution.py:94
  166.1 2.1 %fusion.56 = (f32[1024]{0:T(1024)S(1)}, f32[512]{0:T(512)S(1)}) fusion(f32[64,16,1152]{2,1,0:T(8,128)S(1)} %constant_dynamic-update-slice_fusion, f32[512,512]{1,0:T(8,128)S(1)} %copy-done.19), kind=kOutput, calls=%fused_computation.124 | convolution fusion | flops 1613232640 | bytes 5249024 | tf_op jit(solution)/shard_map/dot_general | solution.py:448
  168.2 18.6 %all-to-all-done.4.moved = bf16[4,2,128,1024]{3,2,1,0:T(8,128)(2,1)} async-done(((bf16[4,2,128,1024]{3,2,1,0:T(8,128)(2,1)}), bf16[4,2,128,1024]{3,2,1,0:T(8,128)(2,1)}, u32[]{:S(2)}, u32[]{:S(2)}) %all-to-all-start.4) | async-done | bytes 2097184 | tf_op jit(solution)/shard_map/all_to_all | solution.py:437
  189.7 3.5 %all-to-all-start.5 = ((f16[8,32,1152]{2,1,0:T(8,128)(2,1)}), f16[8,32,1152]{2,1,0:T(8,128)(2,1)S(1)}, u32[]{:S(2)}, u32[]{:S(2)}) async-start(f16[8,32,1152]{2,1,0:T(8,128)(2,1)} %convert_element_type.62), calls=%async_computation.5 | async-start | bytes 1179648 | tf_op jit(solution)/shard_map/all_to_all | solution.py:438
  193.4 2.9 %multiply_reduce_fusion.1 = (f32[1024]{0:T(1024)S(1)}, f32[1024]{0:T(1024)S(1)}) fusion(f32[64,16,1152]{2,1,0:T(8,128)} %copy-done.20, f32[64,8]{1,0:T(8,128)S(1)} %mul.230, f32[64,8]{1,0:T(8,128)S(1)} %mul.235), kind=kLoop, calls=%fused_computation.14 | loop fusion | flops 4192256 | bytes 4206592 | tf_op jit(solution)/shard_map/reduce_sum | solution.py:456
  197.1 15.3 %all-to-all-done.5 = f16[8,32,1152]{2,1,0:T(8,128)(2,1)S(1)} async-done(((f16[8,32,1152]{2,1,0:T(8,128)(2,1)}), f16[8,32,1152]{2,1,0:T(8,128)(2,1)S(1)}, u32[]{:S(2)}, u32[]{:S(2)}) %all-to-all-start.5) | async-done | bytes 589856 | tf_op jit(solution)/shard_map/all_to_all | solution.py:438
  (160 shorter events, 44.5 us)
Async XLA Ops:
  2.1 19.4 %all-to-all-start = ((bf16[8,16,1024]{2,1,0:T(8,128)(2,1)}), bf16[8,16,1024]{2,1,0:T(8,128)(2,1)S(1)}, u32[]{:S(2)}, u32[]{:S(2)}) async-start(bf16[8,16,1024]{2,1,0:T(8,128)(2,1)} %broadcast_in_dim.10), calls=%async_computation | async-start | bytes 524288 | tf_op jit(solution)/shard_map/all_to_all | solution.py:43
  13.7 55.7 %copy-start.3 = (bf16[1,512,512]{2,1,0:T(8,128)(2,1)}, bf16[1,512,512]{2,1,0:T(8,128)(2,1)S(1)}, u32[]{:S(2)}) copy-start(bf16[1,512,512]{2,1,0:T(8,128)(2,1)S(1)} %copy.41) | copy-start | bytes 1572868
  13.7 29.3 %copy-start.24 = (s32[1,8]{1,0:T(1,128)S(1)}, s32[1,8]{1,0:T(1,128)}, u32[]{:S(2)}) copy-start(s32[1,8]{1,0:T(1,128)} %param.13) | copy-start | bytes 100
  13.7 29.5 %copy-start.25 = (s32[1,8]{1,0:T(1,128)S(1)}, s32[1,8]{1,0:T(1,128)}, u32[]{:S(2)}) copy-start(s32[1,8]{1,0:T(1,128)} %param.12) | copy-start | bytes 100
  13.9 55.4 %copy-start.21 = (bf16[1,512,512]{2,1,0:T(8,128)(2,1)}, bf16[1,512,512]{2,1,0:T(8,128)(2,1)S(1)}, u32[]{:S(2)}) copy-start(bf16[1,512,512]{2,1,0:T(8,128)(2,1)S(1)} %copy.42) | copy-start | bytes 1572868
  22.2 16.7 %all-to-all-start.1 = ((bf16[8,16,1024]{2,1,0:T(8,128)(2,1)}), bf16[8,16,1024]{2,1,0:T(8,128)(2,1)S(1)}, u32[]{:S(2)}, u32[]{:S(2)}) async-start(bf16[8,16,1024]{2,1,0:T(8,128)(2,1)} %broadcast_in_dim.11), calls=%async_computation.1 | async-start | bytes 524288 | tf_op jit(solution)/shard_map/all_to_all | solution.py:43
  25.7 6.6 %collective-permute-start = (bf16[8,16,1024]{2,1,0:T(8,128)(2,1)S(1)}, bf16[8,16,1024]{2,1,0:T(8,128)(2,1)S(1)}, u32[]{:S(2)}, u32[]{:S(2)}) collective-permute-start(bf16[8,16,1024]{2,1,0:T(8,128)(2,1)S(1)} %all-to-all-done.refs_0_), channel_id=1, source_target_pairs={{0,64},{64,128},{128,192},{192,0},{1,65},{65,129},{129,193},{193,1... | collective-permute-start | bytes 786440 | tf_op jit(solution)/shard_map/ppermute | solution.py:51
  27.0 11.8 %collective-permute-start.1 = (bf16[8,16,1024]{2,1,0:T(8,128)(2,1)S(1)}, bf16[8,16,1024]{2,1,0:T(8,128)(2,1)S(1)}, u32[]{:S(2)}, u32[]{:S(2)}) collective-permute-start(bf16[8,16,1024]{2,1,0:T(8,128)(2,1)S(1)} %all-to-all-done.refs_0_), channel_id=1, source_target_pairs={{0,128},{64,192},{128,0},{192,64},{1,129},{65,193},{129,1},{193,65... | collective-permute-start | bytes 786440 | tf_op jit(solution)/shard_map/ppermute | solution.py:51
  29.6 9.3 %collective-permute-start.2 = (bf16[8,16,1024]{2,1,0:T(8,128)(2,1)S(1)}, bf16[8,16,1024]{2,1,0:T(8,128)(2,1)S(1)}, u32[]{:S(2)}, u32[]{:S(2)}) collective-permute-start(bf16[8,16,1024]{2,1,0:T(8,128)(2,1)S(1)} %all-to-all-done.refs_0_), channel_id=1, source_target_pairs={{0,192},{64,0},{128,64},{192,128},{1,193},{65,1},{129,65},{193,129... | collective-permute-start | bytes 786440 | tf_op jit(solution)/shard_map/ppermute | solution.py:51
  39.1 9.4 %collective-permute-start.3 = (bf16[512,1024]{1,0:T(8,128)(2,1)S(1)}, bf16[512,1024]{1,0:T(8,128)(2,1)S(1)}, u32[]{:S(2)}, u32[]{:S(2)}) collective-permute-start(bf16[512,1024]{1,0:T(8,128)(2,1)S(1)} %bitcast.94), channel_id=1, source_target_pairs={{0,4},{4,0},{1,5},{5,1},{2,6},{6,2},{3,7},{7,3},{8,12},{12,8},{9,1... | collective-permute-start | bytes 3145736 | tf_op jit(solution)/shard_map/ppermute | solution.py:47
  43.3 9.1 %collective-permute-start.4 = (bf16[8,16,1024]{2,1,0:T(8,128)(2,1)S(1)}, bf16[8,16,1024]{2,1,0:T(8,128)(2,1)S(1)}, u32[]{:S(2)}, u32[]{:S(2)}) collective-permute-start(bf16[8,16,1024]{2,1,0:T(8,128)(2,1)S(1)} %all-to-all-done.1.refs_0_), channel_id=1, source_target_pairs={{0,64},{64,128},{128,192},{192,0},{1,65},{65,129},{129,193},{193,1... | collective-permute-start | bytes 786440 | tf_op jit(solution)/shard_map/ppermute | solution.py:51
  44.3 14.2 %collective-permute-start.5 = (bf16[8,16,1024]{2,1,0:T(8,128)(2,1)S(1)}, bf16[8,16,1024]{2,1,0:T(8,128)(2,1)S(1)}, u32[]{:S(2)}, u32[]{:S(2)}) collective-permute-start(bf16[8,16,1024]{2,1,0:T(8,128)(2,1)S(1)} %all-to-all-done.1.refs_0_), channel_id=1, source_target_pairs={{0,128},{64,192},{128,0},{192,64},{1,129},{65,193},{129,1},{193,65... | collective-permute-start | bytes 786440 | tf_op jit(solution)/shard_map/ppermute | solution.py:51
  46.4 12.1 %collective-permute-start.6 = (bf16[8,16,1024]{2,1,0:T(8,128)(2,1)S(1)}, bf16[8,16,1024]{2,1,0:T(8,128)(2,1)S(1)}, u32[]{:S(2)}, u32[]{:S(2)}) collective-permute-start(bf16[8,16,1024]{2,1,0:T(8,128)(2,1)S(1)} %all-to-all-done.1.refs_0_), channel_id=1, source_target_pairs={{0,192},{64,0},{128,64},{192,128},{1,193},{65,1},{129,65},{193,129... | collective-permute-start | bytes 786440 | tf_op jit(solution)/shard_map/ppermute | solution.py:51
  58.6 3.4 %collective-permute-start.7 = (bf16[512,1024]{1,0:T(8,128)(2,1)S(1)}, bf16[512,1024]{1,0:T(8,128)(2,1)S(1)}, u32[]{:S(2)}, u32[]{:S(2)}) collective-permute-start(bf16[512,1024]{1,0:T(8,128)(2,1)S(1)} %bitcast.96), channel_id=1, source_target_pairs={{0,4},{4,0},{1,5},{5,1},{2,6},{6,2},{3,7},{7,3},{8,12},{12,8},{9,1... | collective-permute-start | bytes 3145736 | tf_op jit(solution)/shard_map/ppermute | solution.py:47
  65.4 13.6 %collective-permute-start.10 = (f16[128,1024]{1,0:T(8,128)(2,1)}, f16[128,1024]{1,0:T(8,128)(2,1)}, u32[]{:S(2)}, u32[]{:S(2)}) collective-permute-start(f16[128,1024]{1,0:T(8,128)(2,1)} %get-tuple-element.81), channel_id=1, source_target_pairs={{0,3},{1,0},{2,1},{3,2},{4,7},{5,4},{6,5},{7,6},{8,11},{9,8},{10,9... | collective-permute-start | bytes 786440 | tf_op jit(solution)/shard_map/ppermute | solution.py:51
  67.9 11.1 %collective-permute-start.9 = (f16[128,1024]{1,0:T(8,128)(2,1)}, f16[128,1024]{1,0:T(8,128)(2,1)}, u32[]{:S(2)}, u32[]{:S(2)}) collective-permute-start(f16[128,1024]{1,0:T(8,128)(2,1)} %get-tuple-element.82), channel_id=1, source_target_pairs={{0,2},{1,3},{2,0},{3,1},{4,6},{5,7},{6,4},{7,5},{8,10},{9,11},{10,... | collective-permute-start | bytes 786440 | tf_op jit(solution)/shard_map/ppermute | solution.py:51
  68.4 15.1 %collective-permute-start.8 = (f16[128,1024]{1,0:T(8,128)(2,1)S(1)}, f16[128,1024]{1,0:T(8,128)(2,1)}, u32[]{:S(2)}, u32[]{:S(2)}) collective-permute-start(f16[128,1024]{1,0:T(8,128)(2,1)S(1)} %get-tuple-element.80), channel_id=1, source_target_pairs={{0,1},{1,2},{2,3},{3,0},{4,5},{5,6},{6,7},{7,4},{8,9},{9,10},{10,1... | collective-permute-start | bytes 786440 | tf_op jit(solution)/shard_map/ppermute | solution.py:51
  86.0 29.3 %copy-start.8 = (bf16[128,1024]{1,0:T(8,128)(2,1)}, bf16[128,1024]{1,0:T(8,128)(2,1)S(1)}, u32[]{:S(2)}) copy-start(bf16[128,1024]{1,0:T(8,128)(2,1)S(1)} %get-tuple-element.50.own) | copy-start | bytes 786436
  86.5 3.2 %collective-permute-start.13 = (f32[16,1024]{1,0:T(8,128)S(1)}, f32[16,1024]{1,0:T(8,128)S(1)}, u32[]{:S(2)}, u32[]{:S(2)}) collective-permute-start(f32[16,1024]{1,0:T(8,128)S(1)} %fusion.21), channel_id=1, source_target_pairs={{0,3},{1,0},{2,1},{3,2},{4,7},{5,4},{6,5},{7,6},{8,11},{9,8},{10,9... | collective-permute-start | bytes 196616 | tf_op jit(solution)/shard_map/ppermute | solution.py:51
  86.6 4.7 %collective-permute-start.12 = (f32[16,1024]{1,0:T(8,128)S(1)}, f32[16,1024]{1,0:T(8,128)S(1)}, u32[]{:S(2)}, u32[]{:S(2)}) collective-permute-start(f32[16,1024]{1,0:T(8,128)S(1)} %fusion.21), channel_id=1, source_target_pairs={{0,2},{1,3},{2,0},{3,1},{4,6},{5,7},{6,4},{7,5},{8,10},{9,11},{10,... | collective-permute-start | bytes 196616 | tf_op jit(solution)/shard_map/ppermute | solution.py:51
  87.2 5.2 %collective-permute-start.11 = (f32[16,1024]{1,0:T(8,128)S(1)}, f32[16,1024]{1,0:T(8,128)S(1)}, u32[]{:S(2)}, u32[]{:S(2)}) collective-permute-start(f32[16,1024]{1,0:T(8,128)S(1)} %fusion.21), channel_id=1, source_target_pairs={{0,1},{1,2},{2,3},{3,0},{4,5},{5,6},{6,7},{7,4},{8,9},{9,10},{10,1... | collective-permute-start | bytes 196616 | tf_op jit(solution)/shard_map/ppermute | solution.py:51
  109.5 17.0 %all-to-all-start.3 = ((f16[4,8,16,1152]{3,2,1,0:T(8,128)(2,1)}), f16[4,8,16,1152]{3,2,1,0:T(8,128)(2,1)S(1)}, u32[]{:S(2)}, u32[]{:S(2)}) async-start(f16[4,8,16,1152]{3,2,1,0:T(8,128)(2,1)} %broadcast_in_dim.14), calls=%async_computation.3 | async-start | bytes 2359296 | tf_op jit(solution)/shard_map/all_to_all | solution.py:43
  113.2 8.4 %collective-permute-start.14 = (bf16[128,1024]{1,0:T(8,128)(2,1)S(1)}, bf16[128,1024]{1,0:T(8,128)(2,1)S(1)}, u32[]{:S(2)}, u32[]{:S(2)}) collective-permute-start(bf16[128,1024]{1,0:T(8,128)(2,1)S(1)} %get-tuple-element.50.own), channel_id=1, source_target_pairs={{0,3},{1,0},{2,1},{3,2},{4,7},{5,4},{6,5},{7,6},{8,11},{9,8},{10,9... | collective-permute-start | bytes 786440 | tf_op jit(solution)/shard_map/ppermute | solution.py:51
  115.1 6.8 %collective-permute-start.15 = (bf16[128,1024]{1,0:T(8,128)(2,1)S(1)}, bf16[128,1024]{1,0:T(8,128)(2,1)S(1)}, u32[]{:S(2)}, u32[]{:S(2)}) collective-permute-start(bf16[128,1024]{1,0:T(8,128)(2,1)S(1)} %get-tuple-element.50.own), channel_id=1, source_target_pairs={{0,2},{1,3},{2,0},{3,1},{4,6},{5,7},{6,4},{7,5},{8,10},{9,11},{10,... | collective-permute-start | bytes 786440 | tf_op jit(solution)/shard_map/ppermute | solution.py:51
  115.3 10.5 %collective-permute-start.16 = (bf16[128,1024]{1,0:T(8,128)(2,1)S(1)}, bf16[128,1024]{1,0:T(8,128)(2,1)S(1)}, u32[]{:S(2)}, u32[]{:S(2)}) collective-permute-start(bf16[128,1024]{1,0:T(8,128)(2,1)S(1)} %get-tuple-element.50.own), channel_id=1, source_target_pairs={{0,1},{1,2},{2,3},{3,0},{4,5},{5,6},{6,7},{7,4},{8,9},{9,10},{10,1... | collective-permute-start | bytes 786440 | tf_op jit(solution)/shard_map/ppermute | solution.py:51
  126.5 7.6 %collective-permute-start.17 = (f16[4,8,16,1152]{3,2,1,0:T(8,128)(2,1)S(1)}, f16[4,8,16,1152]{3,2,1,0:T(8,128)(2,1)}, u32[]{:S(2)}, u32[]{:S(2)}) collective-permute-start(f16[4,8,16,1152]{3,2,1,0:T(8,128)(2,1)S(1)} %all-to-all-done.3), channel_id=1, source_target_pairs={{0,4},{4,0},{1,5},{5,1},{2,6},{6,2},{3,7},{7,3},{8,12},{12,8},{9,1... | collective-permute-start | bytes 3538952 | tf_op jit(solution)/shard_map/ppermute | solution.py:47
  131.6 18.7 %collective-permute-start.21 = (bf16[512,1024]{1,0:T(8,128)(2,1)}, bf16[512,1024]{1,0:T(8,128)(2,1)}, u32[]{:S(2)}, u32[]{:S(2)}) collective-permute-start(bf16[512,1024]{1,0:T(8,128)(2,1)} %get-tuple-element.42.d), channel_id=1, source_target_pairs={{0,4},{4,0},{1,5},{5,1},{2,6},{6,2},{3,7},{7,3},{8,12},{12,8},{9,1... | collective-permute-start | bytes 3145736 | tf_op jit(solution)/shard_map/ppermute | solution.py:47
  146.8 4.3 %collective-permute-start.19 = (bf16[512,1024]{1,0:T(8,128)(2,1)S(1)}, bf16[512,1024]{1,0:T(8,128)(2,1)S(1)}, u32[]{:S(2)}, u32[]{:S(2)}) collective-permute-start(bf16[512,1024]{1,0:T(8,128)(2,1)S(1)} %get-tuple-element.55.b), channel_id=1, source_target_pairs={{0,4},{4,0},{1,5},{5,1},{2,6},{6,2},{3,7},{7,3},{8,12},{12,8},{9,1... | collective-permute-start | bytes 3145736 | tf_op jit(solution)/shard_map/ppermute | solution.py:47
  147.3 3.0 %collective-permute-start.18 = (bf16[512,512]{1,0:T(8,128)(2,1)S(1)}, bf16[512,512]{1,0:T(8,128)(2,1)S(1)}, u32[]{:S(2)}, u32[]{:S(2)}) collective-permute-start(bf16[512,512]{1,0:T(8,128)(2,1)S(1)} %bitcast.111), channel_id=1, source_target_pairs={{0,4},{4,0},{1,5},{5,1},{2,6},{6,2},{3,7},{7,3},{8,12},{12,8},{9,1... | collective-permute-start | bytes 1572872 | tf_op jit(solution)/shard_map/ppermute | solution.py:47
  147.4 3.7 %collective-permute-start.20 = (bf16[512,512]{1,0:T(8,128)(2,1)S(1)}, bf16[512,512]{1,0:T(8,128)(2,1)S(1)}, u32[]{:S(2)}, u32[]{:S(2)}) collective-permute-start(bf16[512,512]{1,0:T(8,128)(2,1)S(1)} %get-tuple-element.59), channel_id=1, source_target_pairs={{0,4},{4,0},{1,5},{5,1},{2,6},{6,2},{3,7},{7,3},{8,12},{12,8},{9,1... | collective-permute-start | bytes 1572872 | tf_op jit(solution)/shard_map/ppermute | solution.py:47
  155.7 31.0 %all-to-all-start.4 = ((bf16[4,2,128,1024]{3,2,1,0:T(8,128)(2,1)}), bf16[4,2,128,1024]{3,2,1,0:T(8,128)(2,1)}, u32[]{:S(2)}, u32[]{:S(2)}) async-start(bf16[4,2,128,1024]{3,2,1,0:T(8,128)(2,1)} %copy-done.2), calls=%async_computation.4 | async-start | bytes 4194304 | tf_op jit(solution)/shard_map/all_to_all | solution.py:437
  189.7 22.8 %all-to-all-start.5 = ((f16[8,32,1152]{2,1,0:T(8,128)(2,1)}), f16[8,32,1152]{2,1,0:T(8,128)(2,1)S(1)}, u32[]{:S(2)}, u32[]{:S(2)}) async-start(f16[8,32,1152]{2,1,0:T(8,128)(2,1)} %convert_element_type.62), calls=%async_computation.5 | async-start | bytes 1179648 | tf_op jit(solution)/shard_map/all_to_all | solution.py:438
  (24 other events, 194.1 us)
where the time goes:
time: 214 us; the launch traced here: 213 us
  waiting for transfers between devices  89.5 us (42%)
  starting transfers between devices  52.8 us (25%)
  Pallas kernels  18 us (8%)
  blocking collectives  15.6 us (7%)
  local copies, waits for them, and re-layouts  15.2 us (7%)
  matrix products  13 us (6%)
  other arithmetic  8.04 us (4%)
    ppermute x15, waiting for transfers between devices, shifted(): lax.ppermute(value, axis, [(j, (j + step) % count) for j in range(count)])  43 us
    all_to_all x1, waiting for transfers between devices, shards(): last = scale_rows(lax.all_to_all(pieces, 'y', 0, 0)).astype(f16)  18.6 us
    ppermute x15, starting transfers between devices, shifted(): lax.ppermute(value, axis, [(j, (j + step) % count) for j in range(count)])  17.4 us
    all_to_all x3, starting transfers between devices, spread(): lax.all_to_all(jnp.broadcast_to(value[None], (count,) + value.shape), axi...  16.1 us
    all_to_all x1, blocking collectives, spread(): lax.all_to_all(jnp.broadcast_to(value[None], (count,) + value.shape), axi...  15.6 us
    all_to_all x1, waiting for transfers between devices, shards(): last = lax.all_to_all(last, 'z', 0, 0)  15.3 us
    ppermute x7, starting transfers between devices, other_core(): return lax.ppermute(value, 'core', [(0, 1), (1, 0)])  11 us
    all_to_all x3, waiting for transfers between devices, spread(): lax.all_to_all(jnp.broadcast_to(value[None], (count,) + value.shape), axi...  7.58 us
  transfers between devices with their start and end apart: 27, of which 19 were waited for; matrix products, arithmetic and copies ran while one was open for 9% of the time, Pallas kernels for 6%

commit v1 on v0

--- a/solution.py
+++ b/solution.py
@@ -70,7 +70,7 @@
         out_shape=jax.ShapeDtypeStruct((len(pieces),) + value.shape, value.dtype),
         in_specs=[pl.BlockSpec(memory_space=pltpu.SMEM)] + [vmem] * len(pieces),
         out_specs=vmem,
-        compiler_params=pltpu.CompilerParams(vmem_limit_bytes=16 * 1024 * 1024),
+        compiler_params=pltpu.CompilerParams(vmem_limit_bytes=6 * 1024 * 1024),
         cost_estimate=pl.CostEstimate(flops=0, bytes_accessed=2**21, transcendentals=0),
     )(lax.axis_index(axis).reshape(1).astype(jnp.int32), *pieces)
 
@@ -254,7 +254,7 @@
         out_shape=(shape, shape),
         in_specs=[vmem] * 4,
         out_specs=(vmem, vmem),
-        compiler_params=pltpu.CompilerParams(vmem_limit_bytes=24 * 1024 * 1024),
+        compiler_params=pltpu.CompilerParams(vmem_limit_bytes=12 * 1024 * 1024),
         cost_estimate=pl.CostEstimate(flops=2**31, bytes_accessed=2**16, transcendentals=0),
     )(states, d_upward, d_turned, hidden)
 
@@ -276,7 +276,7 @@
             vmem,
         ],
         out_specs=pl.BlockSpec((1, 2, step, columns), lambda k: (k, 0, 0, 0)),
-        compiler_params=pltpu.CompilerParams(vmem_limit_bytes=24 * 1024 * 1024),
+        compiler_params=pltpu.CompilerParams(vmem_limit_bytes=16 * 1024 * 1024),
         cost_estimate=pl.CostEstimate(flops=2**31, bytes_accessed=2**22, transcendentals=0),
     )(up, down, states, d_upward, d_turned, hidden)
 
@@ -305,7 +305,7 @@
         out_shape=jax.ShapeDtypeStruct((Z, parts * rows // Z, columns + 128), f32),
         in_specs=[vmem],
         out_specs=vmem,
-        compiler_params=pltpu.CompilerParams(vmem_limit_bytes=16 * 1024 * 1024),
+        compiler_params=pltpu.CompilerParams(vmem_limit_bytes=8 * 1024 * 1024),
         cost_estimate=pl.CostEstimate(flops=2**20, bytes_accessed=2**22, transcendentals=0),
     )(moved)
 
@@ -325,7 +325,7 @@
         scratch_shapes=[pltpu.VMEM((count, width), bf16)] * 4
         + [pltpu.VMEM((count, count), f32)] * 2
         + [pltpu.VMEM((listed, count), f32)],
-        compiler_params=pltpu.CompilerParams(vmem_limit_bytes=40 * 1024 * 1024),
+        compiler_params=pltpu.CompilerParams(vmem_limit_bytes=22 * 1024 * 1024),
         cost_estimate=pl.CostEstimate(flops=2**20, bytes_accessed=2**16, transcendentals=0),
     )(scalars, first, second, embed, scale, gain)
 
@@ -339,7 +339,7 @@
         + (jax.ShapeDtypeStruct((half, tokens), bf16),) * 2,
         in_specs=[vmem] * (5 + len(quarters)),
         out_specs=(vmem,) * 3,
-        compiler_params=pltpu.CompilerParams(vmem_limit_bytes=24 * 1024 * 1024),
+        compiler_params=pltpu.CompilerParams(vmem_limit_bytes=14 * 1024 * 1024),
         cost_estimate=pl.CostEstimate(flops=2**20, bytes_accessed=2**16, transcendentals=0),
     )(d_sums, table, *quarters, down_mine, down_theirs, slope)
 

time: 214 us -> 214 us (level)
  no operation moved by 1% of the time
where the time goes in v1:
time: 214 us; the launch traced here: 213 us
  waiting for transfers between devices  89.5 us (42%)
  starting transfers between devices  52.8 us (25%)
  Pallas kernels  18 us (8%)
  blocking collectives  15.6 us (7%)
  local copies, waits for them, and re-layouts  15.2 us (7%)
  matrix products  13 us (6%)
  other arithmetic  8.04 us (4%)
    ppermute x15, waiting for transfers between devices, shifted(): lax.ppermute(value, axis, [(j, (j + step) % count) for j in range(count)])  43 us
    all_to_all x1, waiting for transfers between devices, shards(): last = scale_rows(lax.all_to_all(pieces, 'y', 0, 0)).astype(f16)  18.6 us
    ppermute x15, starting transfers between devices, shifted(): lax.ppermute(value, axis, [(j, (j + step) % count) for j in range(count)])  17.4 us
    all_to_all x3, starting transfers between devices, spread(): lax.all_to_all(jnp.broadcast_to(value[None], (count,) + value.shape), axi...  16.1 us
    all_to_all x1, blocking collectives, spread(): lax.all_to_all(jnp.broadcast_to(value[None], (count,) + value.shape), axi...  15.6 us
    all_to_all x1, waiting for transfers between devices, shards(): last = lax.all_to_all(last, 'z', 0, 0)  15.3 us
    ppermute x7, starting transfers between devices, other_core(): return lax.ppermute(value, 'core', [(0, 1), (1, 0)])  11 us
    all_to_all x3, waiting for transfers between devices, spread(): lax.all_to_all(jnp.broadcast_to(value[None], (count,) + value.shape), axi...  7.58 us
  transfers between devices with their start and end apart: 27, of which 19 were waited for; matrix products, arithmetic and copies ran while one was open for 9% of the time, Pallas kernels for 6%

profile of v1, /device:TPU:1, one launch (start us, length us, event | category | flops | bytes accessed | tf_op | source)
XLA Modules:
  0.0 213.4 jit_solution(12571681847818451739)
XLA Ops:
  2.1 9.0 %all-to-all-start = ((bf16[8,16,1024]{2,1,0:T(8,128)(2,1)}), bf16[8,16,1024]{2,1,0:T(8,128)(2,1)S(1)}, u32[]{:S(2)}, u32[]{:S(2)}) async-start(bf16[8,16,1024]{2,1,0:T(8,128)(2,1)} %broadcast_in_dim.10), calls=%async_computation | async-start | bytes 524288 | tf_op jit(solution)/shard_map/all_to_all | solution.py:43
  13.9 7.6 %all-to-all-done.refs_0_ = bf16[8,16,1024]{2,1,0:T(8,128)(2,1)S(1)} async-done(((bf16[8,16,1024]{2,1,0:T(8,128)(2,1)}), bf16[8,16,1024]{2,1,0:T(8,128)(2,1)S(1)}, u32[]{:S(2)}, u32[]{:S(2)}) %all-to-all-start) | async-done | bytes 262176 | tf_op jit(solution)/shard_map/all_to_all | solution.py:43
  22.2 3.4 %all-to-all-start.1 = ((bf16[8,16,1024]{2,1,0:T(8,128)(2,1)}), bf16[8,16,1024]{2,1,0:T(8,128)(2,1)S(1)}, u32[]{:S(2)}, u32[]{:S(2)}) async-start(bf16[8,16,1024]{2,1,0:T(8,128)(2,1)} %broadcast_in_dim.11), calls=%async_computation.1 | async-start | bytes 524288 | tf_op jit(solution)/shard_map/all_to_all | solution.py:43
  27.0 2.6 %collective-permute-start.1 = (bf16[8,16,1024]{2,1,0:T(8,128)(2,1)S(1)}, bf16[8,16,1024]{2,1,0:T(8,128)(2,1)S(1)}, u32[]{:S(2)}, u32[]{:S(2)}) collective-permute-start(bf16[8,16,1024]{2,1,0:T(8,128)(2,1)S(1)} %all-to-all-done.refs_0_), channel_id=1, source_target_pairs={{0,128},{64,192},{128,0},{192,64},{1,129},{65,193},{129,1},{193,65... | collective-permute-start | bytes 786440 | tf_op jit(solution)/shard_map/ppermute | solution.py:51
  32.2 6.6 %collective-permute-done.1.refs_2_ = bf16[8,16,1024]{2,1,0:T(8,128)(2,1)S(1)} collective-permute-done((bf16[8,16,1024]{2,1,0:T(8,128)(2,1)S(1)}, bf16[8,16,1024]{2,1,0:T(8,128)(2,1)S(1)}, u32[]{:S(2)}, u32[]{:S(2)}) %collective-permute-start.1) | collective-permute-done | bytes 262176 | tf_op jit(solution)/shard_map/ppermute | solution.py:51
  39.1 3.6 %collective-permute-start.3 = (bf16[512,1024]{1,0:T(8,128)(2,1)S(1)}, bf16[512,1024]{1,0:T(8,128)(2,1)S(1)}, u32[]{:S(2)}, u32[]{:S(2)}) collective-permute-start(bf16[512,1024]{1,0:T(8,128)(2,1)S(1)} %bitcast.94), channel_id=1, source_target_pairs={{0,4},{4,0},{1,5},{5,1},{2,6},{6,2},{3,7},{7,3},{8,12},{12,8},{9,1... | collective-permute-start | bytes 3145736 | tf_op jit(solution)/shard_map/ppermute | solution.py:47
  44.3 2.1 collective-permute-start.5
  48.4 2.8 %fusion.3 = (f32[512,1024]{1,0:T(8,128)}, bf16[512,1024]{1,0:T(8,128)(2,1)}) fusion(f32[512,1024]{1,0:T(8,128)S(1)} %fusion.60, bf16[512,512]{1,0:T(8,128)(2,1)S(1)} %bitcast.109, bf16[512,1024]{1,0:T(8,128)(2,1)S(1)} %collective-permute-done.3), kind=kOutput, calls=%fused_computation.4 | convolution fusion | flops 542638080 | bytes 6815744 | tf_op jit(solution)/shard_map/dot_general | solution.py:383
  52.5 6.0 %collective-permute-done.5.refs_2_ = bf16[8,16,1024]{2,1,0:T(8,128)(2,1)S(1)} collective-permute-done((bf16[8,16,1024]{2,1,0:T(8,128)(2,1)S(1)}, bf16[8,16,1024]{2,1,0:T(8,128)(2,1)S(1)}, u32[]{:S(2)}, u32[]{:S(2)}) %collective-permute-start.5) | collective-permute-done | bytes 262176 | tf_op jit(solution)/shard_map/ppermute | solution.py:51
  59.8 2.1 %collective-permute-done.7.down_theirs = bf16[512,1024]{1,0:T(8,128)(2,1)S(1)} collective-permute-done((bf16[512,1024]{1,0:T(8,128)(2,1)S(1)}, bf16[512,1024]{1,0:T(8,128)(2,1)S(1)}, u32[]{:S(2)}, u32[]{:S(2)}) %collective-permute-start.7) | collective-permute-done | bytes 1048608 | tf_op jit(solution)/shard_map/ppermute | solution.py:47
  62.0 2.5 %multiply_convert_fusion.1 = f16[384,1024]{1,0:T(8,128)(2,1)S(1)} fusion(bf16[512,1024]{1,0:T(8,128)(2,1)S(1)} %collective-permute-done.7.down_theirs, bf16[512,1024]{1,0:T(8,128)(2,1)S(1)} %bitcast.97, bf16[512,1024]{1,0:T(8,128)(2,1)} %get-tuple-element.42.d), kind=kOutput, calls=%fused_computation.20 | convolution fusion | flops 810287104 | bytes 3670016 | tf_op jit(solution)/shard_map/dot_general | solution.py:88
  65.4 2.5 %collective-permute-start.10 = (f16[128,1024]{1,0:T(8,128)(2,1)}, f16[128,1024]{1,0:T(8,128)(2,1)}, u32[]{:S(2)}, u32[]{:S(2)}) collective-permute-start(f16[128,1024]{1,0:T(8,128)(2,1)} %get-tuple-element.81), channel_id=1, source_target_pairs={{0,3},{1,0},{2,1},{3,2},{4,7},{5,4},{6,5},{7,6},{8,11},{9,8},{10,9... | collective-permute-start | bytes 786440 | tf_op jit(solution)/shard_map/ppermute | solution.py:51
  69.4 9.6 %collective-permute-done.10 = f16[128,1024]{1,0:T(8,128)(2,1)} collective-permute-done((f16[128,1024]{1,0:T(8,128)(2,1)}, f16[128,1024]{1,0:T(8,128)(2,1)}, u32[]{:S(2)}, u32[]{:S(2)}) %collective-permute-start.10) | collective-permute-done | bytes 262176 | tf_op jit(solution)/shard_map/ppermute | solution.py:51
  79.0 4.6 %collective-permute-done.8 = f16[128,1024]{1,0:T(8,128)(2,1)} collective-permute-done((f16[128,1024]{1,0:T(8,128)(2,1)S(1)}, f16[128,1024]{1,0:T(8,128)(2,1)}, u32[]{:S(2)}, u32[]{:S(2)}) %collective-permute-start.8) | collective-permute-done | bytes 262176 | tf_op jit(solution)/shard_map/ppermute | solution.py:51
  83.6 2.2 %fusion.59 = (f32[128]{0:T(128)S(1)}, f32[128,1024]{1,0:T(8,128)S(1)}) fusion(f16[128,1024]{1,0:T(8,128)(2,1)} %collective-permute-done.10, f16[128,1024]{1,0:T(8,128)(2,1)} %collective-permute-done.9, f16[128,1024]{1,0:T(8,128)(2,1)} %collective-permute-done.8, bf16[512,1024]{1,0:T(8,128)(2,1)S(1)} %collective-permute-done.7.down_theirs, ...), kind=kOutput, calls=%fused_computation.127 | convolution fusion | flops 274595712 | bytes 3932672 | tf_op jit(solution)/shard_map/dot_general | solution.py:88
  92.8 15.6 %all_to_all.30 = f16[8,16,1152]{2,1,0:T(8,128)(2,1)S(1)} all-to-all(f16[8,16,1152]{2,1,0:T(8,128)(2,1)S(1)} %broadcast_in_dim.13), channel_id=1, replica_groups=mesh['y'=4,'z'=8,'core'=2,'grp'=4] {'z'}, dimensions={0} | all-to-all | bytes 589824 | tf_op jit(solution)/shard_map/all_to_all | solution.py:43
  109.5 3.6 %all-to-all-start.3 = ((f16[4,8,16,1152]{3,2,1,0:T(8,128)(2,1)}), f16[4,8,16,1152]{3,2,1,0:T(8,128)(2,1)S(1)}, u32[]{:S(2)}, u32[]{:S(2)}) async-start(f16[4,8,16,1152]{3,2,1,0:T(8,128)(2,1)} %broadcast_in_dim.14), calls=%async_computation.3 | async-start | bytes 2359296 | tf_op jit(solution)/shard_map/all_to_all | solution.py:43
  116.0 5.6 %collective-permute-done.14.next1 = bf16[128,1024]{1,0:T(8,128)(2,1)S(1)} collective-permute-done((bf16[128,1024]{1,0:T(8,128)(2,1)S(1)}, bf16[128,1024]{1,0:T(8,128)(2,1)S(1)}, u32[]{:S(2)}, u32[]{:S(2)}) %collective-permute-start.14) | collective-permute-done | bytes 262176 | tf_op jit(solution)/shard_map/ppermute | solution.py:51
  122.7 3.1 %collective-permute-done.16.next3 = bf16[128,1024]{1,0:T(8,128)(2,1)S(1)} collective-permute-done((bf16[128,1024]{1,0:T(8,128)(2,1)S(1)}, bf16[128,1024]{1,0:T(8,128)(2,1)S(1)}, u32[]{:S(2)}, u32[]{:S(2)}) %collective-permute-start.16) | collective-permute-done | bytes 262176 | tf_op jit(solution)/shard_map/ppermute | solution.py:51
  126.5 5.0 %collective-permute-start.17 = (f16[4,8,16,1152]{3,2,1,0:T(8,128)(2,1)S(1)}, f16[4,8,16,1152]{3,2,1,0:T(8,128)(2,1)}, u32[]{:S(2)}, u32[]{:S(2)}) collective-permute-start(f16[4,8,16,1152]{3,2,1,0:T(8,128)(2,1)S(1)} %all-to-all-done.3), channel_id=1, source_target_pairs={{0,4},{4,0},{1,5},{5,1},{2,6},{6,2},{3,7},{7,3},{8,12},{12,8},{9,1... | collective-permute-start | bytes 3538952 | tf_op jit(solution)/shard_map/ppermute | solution.py:47
  132.0 2.1 %collective-permute-done.17 = f16[4,8,16,1152]{3,2,1,0:T(8,128)(2,1)} collective-permute-done((f16[4,8,16,1152]{3,2,1,0:T(8,128)(2,1)S(1)}, f16[4,8,16,1152]{3,2,1,0:T(8,128)(2,1)}, u32[]{:S(2)}, u32[]{:S(2)}) %collective-permute-start.17) | collective-permute-done | bytes 1179680 | tf_op jit(solution)/shard_map/ppermute | solution.py:47
  136.5 7.1 %shard_map.113 = (f32[512,512]{1,0:T(8,128)S(1)}, f32[8,128]{1,0:T(8,128)S(1)}, f32[16,1024]{1,0:T(8,128)S(1)}) custom-call(s32[2]{0:T(128)S(1)} %pad_add_fusion.1.scalars, f32[32,16,1152]{2,1,0:T(8,128)S(1)} %bitcast_convert_fusion.1.first, f32[32,16,1152]{2,1,0:T(8,128)S(1)} %bitcast_convert_fusion.second, f32[16,1024]{1,0:T(8,128)S(1)} %fusion.31.embed, ...), custom_call_target="tpu_custom_call" | custom-call | flops 1048576 | bytes 65536 | tf_op jit(solution)/shard_map/pallas_call | solution.py:316
  143.8 3.0 %shard_map.114 = (bf16[512,1024]{1,0:T(8,128)(2,1)S(1)}, bf16[512,512]{1,0:T(8,128)(2,1)S(1)}, bf16[512,512]{1,0:T(8,128)(2,1)S(1)}) custom-call(f32[16,1024]{1,0:T(8,128)S(1)} %get-tuple-element.49.d_sums, f32[512,16]{1,0:T(8,128)S(1)} %copy-done.7, bf16[128,1024]{1,0:T(8,128)(2,1)S(1)} %copy-done.9, bf16[128,1024]{1,0:T(8,128)(2,1)S(1)} %copy-done.13, ...), custom_call_target="tpu_custom_call" | custom-call | flops 1048576 | bytes 65536 | tf_op jit(solution)/shard_map/pallas_call | solution.py:336
  147.8 2.5 %shard_map.115 = (f32[512,1024]{1,0:T(8,128)S(1)}, f32[512,1024]{1,0:T(8,128)S(1)}) custom-call(bf16[512,512]{1,0:T(8,128)(2,1)S(1)} %bitcast.102, bf16[512,1024]{1,0:T(8,128)(2,1)S(1)} %get-tuple-element.55.b, bf16[512,512]{1,0:T(8,128)(2,1)S(1)} %get-tuple-element.56.c, bf16[512,1024]{1,0:T(8,128)(2,1)} %get-tuple-element.42.d), custom_call_target="tpu_custom_call" | custom-call | flops 2147483648 | bytes 65536 | tf_op jit(solution)/shard_map/pallas_call | solution.py:252
  151.1 3.2 %shard_map.116 = bf16[4,2,128,1024]{3,2,1,0:T(8,128)(2,1)S(1)} custom-call(f32[512,1024]{1,0:T(8,128)S(1)} %get-tuple-element.57.up, f32[512,1024]{1,0:T(8,128)S(1)} %get-tuple-element.58.down, bf16[512,512]{1,0:T(8,128)(2,1)S(1)} %collective-permute-done.18.a, bf16[512,1024]{1,0:T(8,128)(2,1)S(1)} %collective-permute-done.19.b, ...), custom_call_target="tpu_custom_call" | custom-call | flops 2147483648 | bytes 4194304 | tf_op jit(solution)/shard_map/pallas_call | solution.py:266
  155.7 4.8 %all-to-all-start.4 = ((bf16[4,2,128,1024]{3,2,1,0:T(8,128)(2,1)}), bf16[4,2,128,1024]{3,2,1,0:T(8,128)(2,1)}, u32[]{:S(2)}, u32[]{:S(2)}) async-start(bf16[4,2,128,1024]{3,2,1,0:T(8,128)(2,1)} %copy-done.2), calls=%async_computation.4 | async-start | bytes 4194304 | tf_op jit(solution)/shard_map/all_to_all | solution.py:437
  163.9 2.2 %fusion.8 = f32[512]{0:T(512)S(1)} fusion(f32[512,512]{1,0:T(8,128)S(1)} %copy-done.19, f32[64,16,1152]{2,1,0:T(8,128)S(1)} %constant_dynamic-update-slice_fusion), kind=kOutput, calls=%fused_computation.12 | convolution fusion | flops 1612709376 | bytes 5244928 | tf_op jit(solution)/shard_map/dot_general | solution.py:94
  166.1 2.1 %fusion.56 = (f32[1024]{0:T(1024)S(1)}, f32[512]{0:T(512)S(1)}) fusion(f32[64,16,1152]{2,1,0:T(8,128)S(1)} %constant_dynamic-update-slice_fusion, f32[512,512]{1,0:T(8,128)S(1)} %copy-done.19), kind=kOutput, calls=%fused_computation.124 | convolution fusion | flops 1613232640 | bytes 5249024 | tf_op jit(solution)/shard_map/dot_general | solution.py:448
  168.2 18.6 %all-to-all-done.4.moved = bf16[4,2,128,1024]{3,2,1,0:T(8,128)(2,1)} async-done(((bf16[4,2,128,1024]{3,2,1,0:T(8,128)(2,1)}), bf16[4,2,128,1024]{3,2,1,0:T(8,128)(2,1)}, u32[]{:S(2)}, u32[]{:S(2)}) %all-to-all-start.4) | async-done | bytes 2097184 | tf_op jit(solution)/shard_map/all_to_all | solution.py:437
  189.7 3.5 %all-to-all-start.5 = ((f16[8,32,1152]{2,1,0:T(8,128)(2,1)}), f16[8,32,1152]{2,1,0:T(8,128)(2,1)S(1)}, u32[]{:S(2)}, u32[]{:S(2)}) async-start(f16[8,32,1152]{2,1,0:T(8,128)(2,1)} %convert_element_type.62), calls=%async_computation.5 | async-start | bytes 1179648 | tf_op jit(solution)/shard_map/all_to_all | solution.py:438
  193.4 2.9 %multiply_reduce_fusion.1 = (f32[1024]{0:T(1024)S(1)}, f32[1024]{0:T(1024)S(1)}) fusion(f32[64,16,1152]{2,1,0:T(8,128)} %copy-done.20, f32[64,8]{1,0:T(8,128)S(1)} %mul.230, f32[64,8]{1,0:T(8,128)S(1)} %mul.235), kind=kLoop, calls=%fused_computation.14 | loop fusion | flops 4192256 | bytes 4206592 | tf_op jit(solution)/shard_map/reduce_sum | solution.py:456
  197.1 15.3 %all-to-all-done.5 = f16[8,32,1152]{2,1,0:T(8,128)(2,1)S(1)} async-done(((f16[8,32,1152]{2,1,0:T(8,128)(2,1)}), f16[8,32,1152]{2,1,0:T(8,128)(2,1)S(1)}, u32[]{:S(2)}, u32[]{:S(2)}) %all-to-all-start.5) | async-done | bytes 589856 | tf_op jit(solution)/shard_map/all_to_all | solution.py:438
  (160 shorter events, 44.5 us)
Async XLA Ops:
  2.1 19.4 %all-to-all-start = ((bf16[8,16,1024]{2,1,0:T(8,128)(2,1)}), bf16[8,16,1024]{2,1,0:T(8,128)(2,1)S(1)}, u32[]{:S(2)}, u32[]{:S(2)}) async-start(bf16[8,16,1024]{2,1,0:T(8,128)(2,1)} %broadcast_in_dim.10), calls=%async_computation | async-start | bytes 524288 | tf_op jit(solution)/shard_map/all_to_all | solution.py:43
  13.7 55.7 %copy-start.3 = (bf16[1,512,512]{2,1,0:T(8,128)(2,1)}, bf16[1,512,512]{2,1,0:T(8,128)(2,1)S(1)}, u32[]{:S(2)}) copy-start(bf16[1,512,512]{2,1,0:T(8,128)(2,1)S(1)} %copy.41) | copy-start | bytes 1572868
  13.7 29.3 %copy-start.24 = (s32[1,8]{1,0:T(1,128)S(1)}, s32[1,8]{1,0:T(1,128)}, u32[]{:S(2)}) copy-start(s32[1,8]{1,0:T(1,128)} %param.13) | copy-start | bytes 100
  13.7 29.5 %copy-start.25 = (s32[1,8]{1,0:T(1,128)S(1)}, s32[1,8]{1,0:T(1,128)}, u32[]{:S(2)}) copy-start(s32[1,8]{1,0:T(1,128)} %param.12) | copy-start | bytes 100
  13.9 55.4 %copy-start.21 = (bf16[1,512,512]{2,1,0:T(8,128)(2,1)}, bf16[1,512,512]{2,1,0:T(8,128)(2,1)S(1)}, u32[]{:S(2)}) copy-start(bf16[1,512,512]{2,1,0:T(8,128)(2,1)S(1)} %copy.42) | copy-start | bytes 1572868
  22.2 16.7 %all-to-all-start.1 = ((bf16[8,16,1024]{2,1,0:T(8,128)(2,1)}), bf16[8,16,1024]{2,1,0:T(8,128)(2,1)S(1)}, u32[]{:S(2)}, u32[]{:S(2)}) async-start(bf16[8,16,1024]{2,1,0:T(8,128)(2,1)} %broadcast_in_dim.11), calls=%async_computation.1 | async-start | bytes 524288 | tf_op jit(solution)/shard_map/all_to_all | solution.py:43
  25.7 6.6 %collective-permute-start = (bf16[8,16,1024]{2,1,0:T(8,128)(2,1)S(1)}, bf16[8,16,1024]{2,1,0:T(8,128)(2,1)S(1)}, u32[]{:S(2)}, u32[]{:S(2)}) collective-permute-start(bf16[8,16,1024]{2,1,0:T(8,128)(2,1)S(1)} %all-to-all-done.refs_0_), channel_id=1, source_target_pairs={{0,64},{64,128},{128,192},{192,0},{1,65},{65,129},{129,193},{193,1... | collective-permute-start | bytes 786440 | tf_op jit(solution)/shard_map/ppermute | solution.py:51
  27.0 11.8 %collective-permute-start.1 = (bf16[8,16,1024]{2,1,0:T(8,128)(2,1)S(1)}, bf16[8,16,1024]{2,1,0:T(8,128)(2,1)S(1)}, u32[]{:S(2)}, u32[]{:S(2)}) collective-permute-start(bf16[8,16,1024]{2,1,0:T(8,128)(2,1)S(1)} %all-to-all-done.refs_0_), channel_id=1, source_target_pairs={{0,128},{64,192},{128,0},{192,64},{1,129},{65,193},{129,1},{193,65... | collective-permute-start | bytes 786440 | tf_op jit(solution)/shard_map/ppermute | solution.py:51
  29.6 9.3 %collective-permute-start.2 = (bf16[8,16,1024]{2,1,0:T(8,128)(2,1)S(1)}, bf16[8,16,1024]{2,1,0:T(8,128)(2,1)S(1)}, u32[]{:S(2)}, u32[]{:S(2)}) collective-permute-start(bf16[8,16,1024]{2,1,0:T(8,128)(2,1)S(1)} %all-to-all-done.refs_0_), channel_id=1, source_target_pairs={{0,192},{64,0},{128,64},{192,128},{1,193},{65,1},{129,65},{193,129... | collective-permute-start | bytes 786440 | tf_op jit(solution)/shard_map/ppermute | solution.py:51
  39.1 9.4 %collective-permute-start.3 = (bf16[512,1024]{1,0:T(8,128)(2,1)S(1)}, bf16[512,1024]{1,0:T(8,128)(2,1)S(1)}, u32[]{:S(2)}, u32[]{:S(2)}) collective-permute-start(bf16[512,1024]{1,0:T(8,128)(2,1)S(1)} %bitcast.94), channel_id=1, source_target_pairs={{0,4},{4,0},{1,5},{5,1},{2,6},{6,2},{3,7},{7,3},{8,12},{12,8},{9,1... | collective-permute-start | bytes 3145736 | tf_op jit(solution)/shard_map/ppermute | solution.py:47
  43.3 9.1 %collective-permute-start.4 = (bf16[8,16,1024]{2,1,0:T(8,128)(2,1)S(1)}, bf16[8,16,1024]{2,1,0:T(8,128)(2,1)S(1)}, u32[]{:S(2)}, u32[]{:S(2)}) collective-permute-start(bf16[8,16,1024]{2,1,0:T(8,128)(2,1)S(1)} %all-to-all-done.1.refs_0_), channel_id=1, source_target_pairs={{0,64},{64,128},{128,192},{192,0},{1,65},{65,129},{129,193},{193,1... | collective-permute-start | bytes 786440 | tf_op jit(solution)/shard_map/ppermute | solution.py:51
  44.3 14.2 %collective-permute-start.5 = (bf16[8,16,1024]{2,1,0:T(8,128)(2,1)S(1)}, bf16[8,16,1024]{2,1,0:T(8,128)(2,1)S(1)}, u32[]{:S(2)}, u32[]{:S(2)}) collective-permute-start(bf16[8,16,1024]{2,1,0:T(8,128)(2,1)S(1)} %all-to-all-done.1.refs_0_), channel_id=1, source_target_pairs={{0,128},{64,192},{128,0},{192,64},{1,129},{65,193},{129,1},{193,65... | collective-permute-start | bytes 786440 | tf_op jit(solution)/shard_map/ppermute | solution.py:51
  46.4 12.1 %collective-permute-start.6 = (bf16[8,16,1024]{2,1,0:T(8,128)(2,1)S(1)}, bf16[8,16,1024]{2,1,0:T(8,128)(2,1)S(1)}, u32[]{:S(2)}, u32[]{:S(2)}) collective-permute-start(bf16[8,16,1024]{2,1,0:T(8,128)(2,1)S(1)} %all-to-all-done.1.refs_0_), channel_id=1, source_target_pairs={{0,192},{64,0},{128,64},{192,128},{1,193},{65,1},{129,65},{193,129... | collective-permute-start | bytes 786440 | tf_op jit(solution)/shard_map/ppermute | solution.py:51
  58.6 3.4 %collective-permute-start.7 = (bf16[512,1024]{1,0:T(8,128)(2,1)S(1)}, bf16[512,1024]{1,0:T(8,128)(2,1)S(1)}, u32[]{:S(2)}, u32[]{:S(2)}) collective-permute-start(bf16[512,1024]{1,0:T(8,128)(2,1)S(1)} %bitcast.96), channel_id=1, source_target_pairs={{0,4},{4,0},{1,5},{5,1},{2,6},{6,2},{3,7},{7,3},{8,12},{12,8},{9,1... | collective-permute-start | bytes 3145736 | tf_op jit(solution)/shard_map/ppermute | solution.py:47
  65.4 13.6 %collective-permute-start.10 = (f16[128,1024]{1,0:T(8,128)(2,1)}, f16[128,1024]{1,0:T(8,128)(2,1)}, u32[]{:S(2)}, u32[]{:S(2)}) collective-permute-start(f16[128,1024]{1,0:T(8,128)(2,1)} %get-tuple-element.81), channel_id=1, source_target_pairs={{0,3},{1,0},{2,1},{3,2},{4,7},{5,4},{6,5},{7,6},{8,11},{9,8},{10,9... | collective-permute-start | bytes 786440 | tf_op jit(solution)/shard_map/ppermute | solution.py:51
  67.9 11.1 %collective-permute-start.9 = (f16[128,1024]{1,0:T(8,128)(2,1)}, f16[128,1024]{1,0:T(8,128)(2,1)}, u32[]{:S(2)}, u32[]{:S(2)}) collective-permute-start(f16[128,1024]{1,0:T(8,128)(2,1)} %get-tuple-element.82), channel_id=1, source_target_pairs={{0,2},{1,3},{2,0},{3,1},{4,6},{5,7},{6,4},{7,5},{8,10},{9,11},{10,... | collective-permute-start | bytes 786440 | tf_op jit(solution)/shard_map/ppermute | solution.py:51
  68.4 15.1 %collective-permute-start.8 = (f16[128,1024]{1,0:T(8,128)(2,1)S(1)}, f16[128,1024]{1,0:T(8,128)(2,1)}, u32[]{:S(2)}, u32[]{:S(2)}) collective-permute-start(f16[128,1024]{1,0:T(8,128)(2,1)S(1)} %get-tuple-element.80), channel_id=1, source_target_pairs={{0,1},{1,2},{2,3},{3,0},{4,5},{5,6},{6,7},{7,4},{8,9},{9,10},{10,1... | collective-permute-start | bytes 786440 | tf_op jit(solution)/shard_map/ppermute | solution.py:51
  86.0 29.3 %copy-start.8 = (bf16[128,1024]{1,0:T(8,128)(2,1)}, bf16[128,1024]{1,0:T(8,128)(2,1)S(1)}, u32[]{:S(2)}) copy-start(bf16[128,1024]{1,0:T(8,128)(2,1)S(1)} %get-tuple-element.50.own) | copy-start | bytes 786436
  86.5 3.2 %collective-permute-start.13 = (f32[16,1024]{1,0:T(8,128)S(1)}, f32[16,1024]{1,0:T(8,128)S(1)}, u32[]{:S(2)}, u32[]{:S(2)}) collective-permute-start(f32[16,1024]{1,0:T(8,128)S(1)} %fusion.21), channel_id=1, source_target_pairs={{0,3},{1,0},{2,1},{3,2},{4,7},{5,4},{6,5},{7,6},{8,11},{9,8},{10,9... | collective-permute-start | bytes 196616 | tf_op jit(solution)/shard_map/ppermute | solution.py:51
  86.6 4.7 %collective-permute-start.12 = (f32[16,1024]{1,0:T(8,128)S(1)}, f32[16,1024]{1,0:T(8,128)S(1)}, u32[]{:S(2)}, u32[]{:S(2)}) collective-permute-start(f32[16,1024]{1,0:T(8,128)S(1)} %fusion.21), channel_id=1, source_target_pairs={{0,2},{1,3},{2,0},{3,1},{4,6},{5,7},{6,4},{7,5},{8,10},{9,11},{10,... | collective-permute-start | bytes 196616 | tf_op jit(solution)/shard_map/ppermute | solution.py:51
  87.2 5.2 %collective-permute-start.11 = (f32[16,1024]{1,0:T(8,128)S(1)}, f32[16,1024]{1,0:T(8,128)S(1)}, u32[]{:S(2)}, u32[]{:S(2)}) collective-permute-start(f32[16,1024]{1,0:T(8,128)S(1)} %fusion.21), channel_id=1, source_target_pairs={{0,1},{1,2},{2,3},{3,0},{4,5},{5,6},{6,7},{7,4},{8,9},{9,10},{10,1... | collective-permute-start | bytes 196616 | tf_op jit(solution)/shard_map/ppermute | solution.py:51
  109.5 17.0 %all-to-all-start.3 = ((f16[4,8,16,1152]{3,2,1,0:T(8,128)(2,1)}), f16[4,8,16,1152]{3,2,1,0:T(8,128)(2,1)S(1)}, u32[]{:S(2)}, u32[]{:S(2)}) async-start(f16[4,8,16,1152]{3,2,1,0:T(8,128)(2,1)} %broadcast_in_dim.14), calls=%async_computation.3 | async-start | bytes 2359296 | tf_op jit(solution)/shard_map/all_to_all | solution.py:43
  113.2 8.4 %collective-permute-start.14 = (bf16[128,1024]{1,0:T(8,128)(2,1)S(1)}, bf16[128,1024]{1,0:T(8,128)(2,1)S(1)}, u32[]{:S(2)}, u32[]{:S(2)}) collective-permute-start(bf16[128,1024]{1,0:T(8,128)(2,1)S(1)} %get-tuple-element.50.own), channel_id=1, source_target_pairs={{0,3},{1,0},{2,1},{3,2},{4,7},{5,4},{6,5},{7,6},{8,11},{9,8},{10,9... | collective-permute-start | bytes 786440 | tf_op jit(solution)/shard_map/ppermute | solution.py:51
  115.1 6.8 %collective-permute-start.15 = (bf16[128,1024]{1,0:T(8,128)(2,1)S(1)}, bf16[128,1024]{1,0:T(8,128)(2,1)S(1)}, u32[]{:S(2)}, u32[]{:S(2)}) collective-permute-start(bf16[128,1024]{1,0:T(8,128)(2,1)S(1)} %get-tuple-element.50.own), channel_id=1, source_target_pairs={{0,2},{1,3},{2,0},{3,1},{4,6},{5,7},{6,4},{7,5},{8,10},{9,11},{10,... | collective-permute-start | bytes 786440 | tf_op jit(solution)/shard_map/ppermute | solution.py:51
  115.3 10.5 %collective-permute-start.16 = (bf16[128,1024]{1,0:T(8,128)(2,1)S(1)}, bf16[128,1024]{1,0:T(8,128)(2,1)S(1)}, u32[]{:S(2)}, u32[]{:S(2)}) collective-permute-start(bf16[128,1024]{1,0:T(8,128)(2,1)S(1)} %get-tuple-element.50.own), channel_id=1, source_target_pairs={{0,1},{1,2},{2,3},{3,0},{4,5},{5,6},{6,7},{7,4},{8,9},{9,10},{10,1... | collective-permute-start | bytes 786440 | tf_op jit(solution)/shard_map/ppermute | solution.py:51
  126.5 7.6 %collective-permute-start.17 = (f16[4,8,16,1152]{3,2,1,0:T(8,128)(2,1)S(1)}, f16[4,8,16,1152]{3,2,1,0:T(8,128)(2,1)}, u32[]{:S(2)}, u32[]{:S(2)}) collective-permute-start(f16[4,8,16,1152]{3,2,1,0:T(8,128)(2,1)S(1)} %all-to-all-done.3), channel_id=1, source_target_pairs={{0,4},{4,0},{1,5},{5,1},{2,6},{6,2},{3,7},{7,3},{8,12},{12,8},{9,1... | collective-permute-start | bytes 3538952 | tf_op jit(solution)/shard_map/ppermute | solution.py:47
  131.6 18.7 %collective-permute-start.21 = (bf16[512,1024]{1,0:T(8,128)(2,1)}, bf16[512,1024]{1,0:T(8,128)(2,1)}, u32[]{:S(2)}, u32[]{:S(2)}) collective-permute-start(bf16[512,1024]{1,0:T(8,128)(2,1)} %get-tuple-element.42.d), channel_id=1, source_target_pairs={{0,4},{4,0},{1,5},{5,1},{2,6},{6,2},{3,7},{7,3},{8,12},{12,8},{9,1... | collective-permute-start | bytes 3145736 | tf_op jit(solution)/shard_map/ppermute | solution.py:47
  146.8 4.3 %collective-permute-start.19 = (bf16[512,1024]{1,0:T(8,128)(2,1)S(1)}, bf16[512,1024]{1,0:T(8,128)(2,1)S(1)}, u32[]{:S(2)}, u32[]{:S(2)}) collective-permute-start(bf16[512,1024]{1,0:T(8,128)(2,1)S(1)} %get-tuple-element.55.b), channel_id=1, source_target_pairs={{0,4},{4,0},{1,5},{5,1},{2,6},{6,2},{3,7},{7,3},{8,12},{12,8},{9,1... | collective-permute-start | bytes 3145736 | tf_op jit(solution)/shard_map/ppermute | solution.py:47
  147.3 3.0 %collective-permute-start.18 = (bf16[512,512]{1,0:T(8,128)(2,1)S(1)}, bf16[512,512]{1,0:T(8,128)(2,1)S(1)}, u32[]{:S(2)}, u32[]{:S(2)}) collective-permute-start(bf16[512,512]{1,0:T(8,128)(2,1)S(1)} %bitcast.111), channel_id=1, source_target_pairs={{0,4},{4,0},{1,5},{5,1},{2,6},{6,2},{3,7},{7,3},{8,12},{12,8},{9,1... | collective-permute-start | bytes 1572872 | tf_op jit(solution)/shard_map/ppermute | solution.py:47
  147.4 3.7 %collective-permute-start.20 = (bf16[512,512]{1,0:T(8,128)(2,1)S(1)}, bf16[512,512]{1,0:T(8,128)(2,1)S(1)}, u32[]{:S(2)}, u32[]{:S(2)}) collective-permute-start(bf16[512,512]{1,0:T(8,128)(2,1)S(1)} %get-tuple-element.59), channel_id=1, source_target_pairs={{0,4},{4,0},{1,5},{5,1},{2,6},{6,2},{3,7},{7,3},{8,12},{12,8},{9,1... | collective-permute-start | bytes 1572872 | tf_op jit(solution)/shard_map/ppermute | solution.py:47
  155.7 31.0 %all-to-all-start.4 = ((bf16[4,2,128,1024]{3,2,1,0:T(8,128)(2,1)}), bf16[4,2,128,1024]{3,2,1,0:T(8,128)(2,1)}, u32[]{:S(2)}, u32[]{:S(2)}) async-start(bf16[4,2,128,1024]{3,2,1,0:T(8,128)(2,1)} %copy-done.2), calls=%async_computation.4 | async-start | bytes 4194304 | tf_op jit(solution)/shard_map/all_to_all | solution.py:437
  189.7 22.8 %all-to-all-start.5 = ((f16[8,32,1152]{2,1,0:T(8,128)(2,1)}), f16[8,32,1152]{2,1,0:T(8,128)(2,1)S(1)}, u32[]{:S(2)}, u32[]{:S(2)}) async-start(f16[8,32,1152]{2,1,0:T(8,128)(2,1)} %convert_element_type.62), calls=%async_computation.5 | async-start | bytes 1179648 | tf_op jit(solution)/shard_map/all_to_all | solution.py:438
  (24 other events, 194.1 us)
